TPU v7x, 256 devices: a whole 4x4x8 slice. The times are simulated.
256 devices in a mesh: dp: 16 (over y_lo, z), seq: 16 (over x, y_hi, core).
Axes of the slice: x: 4, y: 4 (y_hi: 2, y_lo: 2; y = y_hi * 2 + y_lo), z: 8, core: 2. Of those that a mesh axis runs over, the one named last changes fastest.
Arguments:
- tokens: bfloat16 [16, 4096, 1536], P('dp', 'seq'), may hold values from -64 to 64
- keep_index: int32 [16, 4096], P('dp', 'seq'), may hold values from 0 to 8191, as said below
- d_out: bfloat16 [16, 4096, 768], P('dp', 'seq'), may hold values from -6 to 6
- w_query: bfloat16 [1536, 768], replicated, may hold values from -0.15625 to 0.15625
- w_kv: bfloat16 [1536, 1536], replicated, may hold values from -0.15625 to 0.15625
- w_merge: float32 [4, 1536], replicated, may hold values from -2.5 to 2.5
Outputs:
- attended: bfloat16 [16, 4096, 768], P('dp', 'seq')
- grad_tokens: bfloat16 [16, 4096, 1536], P('dp', 'seq')
- grad_query_w: float32 [1536, 768], P('seq')
- grad_kv_w: float32 [1536, 1536], P('seq')
- grad_merge: float32 [4, 1536], P(None, 'seq')
Inputs may be any that keep to these rules, and one draw needn't show every extreme that they name: `keep_index`: for each image: ascending and distinct; made of whole aligned blocks of 128 positions, 32 of the 64 blocks, the first and the last block always among them.
All inputs are finite; a program needn't handle non-finite values.
Results may differ from a plain program's by a relative error of at most 0.034.
The roundings to bfloat16 on the way count: a program that leaves them out, or rounds other values in their place, can miss the bound.
Values may be sent and summed in bfloat16 or wider, within the bound.
No kernel may reach another device: no remote copies, remote signals or barrier semaphores. Data moves between devices by JAX's collectives and lax.ppermute only.
A program may use at most 128 MiB of HBM per device.

v0:
```python
import jax
import jax.numpy as jnp
import numpy as np
from jax import lax
from jax.experimental import pallas as pl
from jax.experimental.pallas import tpu as pltpu
from jax.sharding import PartitionSpec as P

D = 1536
HD = 768
HEADS = 12
HEAD = 64
GROUP = 192
ROWS = 384
TOK = 256
CELLS = 64
MSG = 400
FREQ = (100.0 ** (-np.arange(16, dtype=np.float64) / 16)).astype(np.float32)
F32 = jnp.float32
BF16 = jnp.bfloat16

X_SHIFT = [[(i, (((i >> 2) + k) % 4) * 4 + (i & 3)) for i in range(16)] for k in range(4)]
Y_SWAP = [(i, i ^ 2) for i in range(16)]
CORE_SWAP = [(i, i ^ 1) for i in range(16)]
YLO_SWAP = [(i, i ^ 8) for i in range(16)]
Z_GROUPS = [list(range(8)), list(range(8, 16))]


def params(mib):
    return pltpu.CompilerParams(vmem_limit_bytes=mib * 1024 * 1024)


def cost(us):
    return pl.CostEstimate(flops=int(us * 1.1e9), bytes_accessed=int(us * 1e5), transcendentals=0)


def vmem():
    return pl.BlockSpec(memory_space=pltpu.VMEM)


def smem():
    return pl.BlockSpec(memory_space=pltpu.SMEM)


def mm(a, b, dims=((1,), (0,))):
    return lax.dot_general(a, b, (dims, ((), ())), preferred_element_type=F32)


def frequency(shape, axis):
    j = lax.broadcasted_iota(jnp.int32, shape, axis) & 15
    freq = jnp.zeros(shape, F32)
    for k in range(16):
        freq = jnp.where(j == k, float(FREQ[k]), freq)
    return freq


def hbm():
    return pl.BlockSpec(memory_space=pltpu.MemorySpace.HBM)


def lane_tables(row, col, sign):
    lane = lax.broadcasted_iota(jnp.int32, row.shape, 1)
    angle = jnp.where((lane & 63) < 32, row, col)
    even = (lane & 31) < 16
    return jnp.cos(angle), jnp.sin(angle) * jnp.where(even, -sign, sign), even


def turn(u, cos, sin, even):
    swapped = jnp.where(even, pltpu.roll(u, 112, 1), pltpu.roll(u, 16, 1))
    return u * cos + swapped * sin


def merge(tokf, wm_ref, k, cells):
    total = None
    for t in range(4):
        one = tokf[k, pl.ds(t, cells, stride=4), :] * wm_ref[t : t + 1, pl.ds(128 * k, 128)]
        total = one if total is None else total + one
    return total


def keyval_kernel(x_ref, idx_ref, tok_hbm, wm_hbm, wkv_ref, o0, o1, o2, o3, tok_ref, wm_ref, tokf, merged, weights, piece, sems):
    copies = [pltpu.make_async_copy(wkv_ref.at[:, pl.ds(512 * j, 512)], weights.at[j], sems.at[j]) for j in range(3)]
    first = [pltpu.make_async_copy(tok_hbm, tok_ref, sems.at[3]), pltpu.make_async_copy(wm_hbm, wm_ref, sems.at[4])]
    for one in first + copies:
        one.start()
    freq = frequency((1, 128), 1)
    i = lax.broadcasted_iota(jnp.int32, (CELLS, 128), 0)
    start = idx_ref[0] // 4
    second = idx_ref[128] // 4
    cell = jnp.where(i < 32, start + i, second + i - 32)
    row = (2 * (cell >> 6)).astype(F32) + 0.5
    col = (2 * (cell & 63)).astype(F32) + 0.5
    cos, sin, even = lane_tables(row * freq, col * freq, 1.0)
    left = lax.broadcasted_iota(jnp.int32, (CELLS, 128), 1) < 64
    for one in first:
        one.wait()
    for k in range(12):
        tokf[k] = tok_ref[:, pl.ds(128 * k, 128)].astype(F32)
        merged[:, pl.ds(128 * k, 128)] = merge(tokf, wm_ref, k, CELLS).astype(BF16)
    tiles = []
    for j in range(3):
        copies[j].wait()
        part = mm(merged[...], weights[j])
        tiles += [part[:, 128 * k : 128 * k + 128] for k in range(4)]
    for k in range(6):
        key = turn(tiles[k], cos, sin, even)
        val = tiles[6 + k]
        a = jnp.where(left, key, pltpu.roll(val, 64, 1)).astype(BF16)
        b = jnp.where(left, pltpu.roll(key, 64, 1), val).astype(BF16)
        piece[(2 * k) // 3, (2 * k) % 3] = a
        piece[(2 * k + 1) // 3, (2 * k + 1) % 3] = b
    x = x_ref[0]
    for d, out in enumerate((o0, o1, o2, o3)):
        out[...] = piece[(x + d) % 4]


def keyval(xs, index, tokens, w_merge, w_kv):
    out = jax.ShapeDtypeStruct((3, CELLS, 128), BF16)
    return pl.pallas_call(
        keyval_kernel,
        in_specs=[smem(), smem(), hbm(), hbm(), hbm()],
        out_specs=[vmem()] * 4,
        out_shape=[out] * 4,
        scratch_shapes=[
            pltpu.VMEM((TOK, D), BF16),
            pltpu.VMEM((4, D), F32),
            pltpu.VMEM((12, TOK, 128), F32),
            pltpu.VMEM((CELLS, D), BF16),
            pltpu.VMEM((3, D, 512), BF16),
            pltpu.VMEM((4, 3, CELLS, 128), BF16),
            pltpu.SemaphoreType.DMA((5,)),
        ],
        compiler_params=params(56),
        cost_estimate=cost(6),
        name="keyval",
    )(xs, index, tokens, w_merge, w_kv)


def sub_tables(row, col, freq):
    return (
        jnp.cos(row * freq),
        jnp.sin(row * freq),
        jnp.cos(col * freq),
        jnp.sin(col * freq),
    )


def sub_turn(u, tables, sign):
    rc, rs, cc, cs = tables
    a, b, c, d = u[0:16], u[16:32], u[32:48], u[48:64]
    return jnp.concatenate(
        [
            a * rc - sign * (b * rs),
            sign * (a * rs) + b * rc,
            c * cc - sign * (d * cs),
            sign * (c * cs) + d * cc,
        ],
        axis=0,
    )


def query_kernel(x_ref, idx_ref, tok_ref, wq_ref, do_ref, o0, o1, o2, o3, scr):
    index = idx_ref[...]
    cell = index >> 2
    row = 2 * (cell >> 6) + ((index >> 1) & 1)
    col = 2 * (cell & 63) + (index & 1)
    row = row.astype(F32)
    col = col.astype(F32)
    tables = sub_tables(row, col, frequency((16, TOK), 0))
    query = mm(tok_ref[...], wq_ref[...]).T
    same = lax.broadcasted_iota(jnp.int32, (TOK, TOK), 0) == lax.broadcasted_iota(jnp.int32, (TOK, TOK), 1)
    same = jnp.where(same, 1.0, 0.0).astype(BF16)
    grad = [mm(same, do_ref[:, pl.ds(256 * k, 256)], ((1,), (1,))).astype(BF16) for k in range(3)]
    grad = jnp.concatenate(grad, axis=0)
    line = lax.broadcasted_iota(jnp.int32, (16, TOK), 0)
    place = jnp.where(line == 0, row, jnp.where(line == 1, col, 0.0)).astype(BF16)
    for h in range(HEADS):
        g, k = h // 3, h % 3
        scr[g, pl.ds(64 * k, 64), :] = (sub_turn(query[64 * h : 64 * h + 64], tables, 1.0) * 0.125).astype(BF16)
    for g in range(4):
        scr[g, pl.ds(GROUP, GROUP), :] = grad[GROUP * g : GROUP * g + GROUP]
        scr[g, pl.ds(2 * GROUP, 16), :] = place
    x = x_ref[0]
    for d, out in enumerate((o0, o1, o2, o3)):
        out[...] = scr[(x + d) % 4]


def queries(xs, index, tokens, w_query, grad):
    out = jax.ShapeDtypeStruct((MSG, TOK), BF16)
    return pl.pallas_call(
        query_kernel,
        in_specs=[smem()] + [vmem()] * 4,
        out_specs=[vmem()] * 4,
        out_shape=[out] * 4,
        scratch_shapes=[pltpu.VMEM((4, MSG, TOK), BF16)],
        compiler_params=params(8),
        cost_estimate=cost(4),
        name="queries",
    )(xs, index, tokens, w_query, grad)


def attention_kernel(
    x_ref, q0, q1, q2, q3, u0, u1, u2, u3, a0, a1, a2, a3, dq_ref, keep_ref, send_ref, kvn, kvt, qd, att, tables
):
    x = x_ref[0]
    for k, u in enumerate((u0, u1, u2, u3)):
        for d in range(4):
            for h in range(3):
                kvn[h, pl.ds(256 * k + 64 * d, 64), :] = u[d, h]
    for h in range(3):
        kvt[h] = kvn[h].astype(F32).T.astype(BF16)
    for d, q in enumerate((q0, q1, q2, q3)):
        qd[d] = q[...]

    freq = frequency((16, TOK), 0)
    for p in range(4):
        place = qd[p, pl.ds(2 * GROUP, 16), :].astype(F32)
        for k, table in enumerate(sub_tables(place[0:1], place[1:2], freq)):
            tables[p, pl.ds(16 * k, 16), :] = table

    def step(h, carry):
        at = pl.ds(pl.multiple_of(64 * h, 64), 64)
        kv = kvn[h]
        kv_t = kvt[h]
        total = None
        outs = []
        for p in range(4):
            q = qd[p, at, :]
            do = qd[p, pl.ds(pl.multiple_of(GROUP + 64 * h, 64), 64), :]
            zero = jnp.zeros_like(q)
            q_pad = jnp.concatenate([q, zero], axis=0)
            do_pad = jnp.concatenate([zero, do], axis=0)
            scores = mm(kv, q_pad)
            top = jnp.max(scores, axis=0, keepdims=True)
            expo = jnp.exp(scores - top)
            denom = jnp.sum(expo, axis=0, keepdims=True)
            inv = 1.0 / denom
            mixed = mm(kv_t[64:128], expo.astype(BF16)) * inv
            mixed = mixed.astype(BF16)
            delta = jnp.sum(mixed.astype(F32) * do.astype(F32), axis=0, keepdims=True)
            prob = expo * inv
            dprob = mm(kv, do_pad)
            dscore = (prob * (dprob - delta)).astype(BF16)
            dq = mm(kv_t[0:64], dscore) * 0.125
            table = [tables[p, pl.ds(16 * k, 16), :] for k in range(4)]
            outs.append((mixed, sub_turn(dq, table, -1.0).astype(BF16)))
            part = mm(dscore, q_pad, ((1,), (1,))) + mm(prob.astype(BF16), do_pad, ((1,), (1,)))
            total = part if total is None else total + part
        for p, (mixed, dq) in enumerate(outs):
            att[p, at, :] = mixed
            dq_ref[(x + 4 - p) % 4, at, :] = dq
        keep_ref[h] = total[0:512]
        send_ref[h] = total[512:1024].astype(BF16)
        return carry

    lax.fori_loop(0, 3, step, 0)
    for d, a in enumerate((a0, a1, a2, a3)):
        a[...] = att[d]


def attention(xs, qs, us):
    out = jax.ShapeDtypeStruct((GROUP, TOK), BF16)
    return pl.pallas_call(
        attention_kernel,
        in_specs=[smem()] + [vmem()] * 8,
        out_specs=[vmem()] * 7,
        out_shape=[out] * 4
        + [
            jax.ShapeDtypeStruct((4, GROUP, TOK), BF16),
            jax.ShapeDtypeStruct((3, 512, 128), F32),
            jax.ShapeDtypeStruct((3, 512, 128), BF16),
        ],
        scratch_shapes=[
            pltpu.VMEM((3, 1024, 128), BF16),
            pltpu.VMEM((3, 128, 1024), BF16),
            pltpu.VMEM((4, MSG, TOK), BF16),
            pltpu.VMEM((4, GROUP, TOK), BF16),
            pltpu.VMEM((4, 64, TOK), F32),
        ],
        compiler_params=params(56),
        cost_estimate=cost(20),
        name="attention",
    )(xs, *qs, *us)


def table_kernel(q0, q1, q2, q3, cos_ref, sin_ref):
    freq = frequency((1, 128), 1)
    i = lax.broadcasted_iota(jnp.int32, (32, 128), 0).astype(F32)
    left = lax.broadcasted_iota(jnp.int32, (32, 128), 1) < 64
    for d, q in enumerate((q0, q1, q2, q3)):
        place = q[pl.ds(2 * GROUP, 16), :].astype(F32)
        for b in range(2):
            row = jnp.broadcast_to(place[0:1, 128 * b : 128 * b + 1], (32, 128)) + 0.5
            col = jnp.broadcast_to(place[1:2, 128 * b : 128 * b + 1], (32, 128)) + 0.5 + 2.0 * i
            cos, sin, even = lane_tables(row * freq, col * freq, -1.0)
            at = pl.ds(64 * d + 32 * b, 32)
            cos_ref[at, :] = jnp.where(left, cos, 1.0)
            sin_ref[at, :] = jnp.where(left, sin, 0.0)


def key_tables(qs):
    out = jax.ShapeDtypeStruct((TOK, 128), F32)
    return pl.pallas_call(
        table_kernel,
        in_specs=[vmem()] * 4,
        out_specs=[vmem()] * 2,
        out_shape=[out] * 2,
        compiler_params=params(56),
        cost_estimate=cost(2),
        name="key_tables",
    )(*qs)


def dkv_kernel(x_ref, cos_ref, sin_ref, keep_ref, core_ref, y_ref, out_ref):
    x = x_ref[0]
    even = (lax.broadcasted_iota(jnp.int32, (CELLS, 128), 1) & 31) < 16
    for d in range(4):
        at = pl.ds(64 * d, 64)
        for h in range(3):
            total = keep_ref[h, at, :] + core_ref[h, at, :].astype(F32) + y_ref[h, at, :].astype(F32)
            out_ref[(x + 4 - d) % 4, h] = turn(total, cos_ref[at, :], sin_ref[at, :], even).astype(BF16)


def finish_dkv(xs, tables, keep, core, y):
    half = pl.BlockSpec((3, 256, 128), lambda i: (0, 0, 0))
    return pl.pallas_call(
        dkv_kernel,
        grid=(1,),
        in_specs=[smem(), pl.BlockSpec((TOK, 128), lambda i: (0, 0)), pl.BlockSpec((TOK, 128), lambda i: (0, 0)), half, half, half],
        out_specs=pl.BlockSpec((4, 3, CELLS, 128), lambda i: (0, 0, 0, 0)),
        out_shape=jax.ShapeDtypeStruct((4, 3, CELLS, 128), BF16),
        compiler_params=params(56),
        cost_estimate=cost(2),
        name="finish_dkv",
    )(xs, *tables, keep, core, y)


def term_q_kernel(x_ref, c_ref, t0, t1, t2, t3, d0, d1, d2, d3, wm_ref, keep_ref, send_ref, tokf, merged_ref, scr, rows):
    x = x_ref[0]
    toks = (t0, t1, t2, t3)
    for d, t in enumerate(toks):
        for k in range(3):
            tokf[k, pl.ds(256 * d, 256), :] = t[:, pl.ds(128 * k, 128)].astype(F32)
    merged_ref[...] = jnp.concatenate([merge(tokf, wm_ref, k, 256) for k in range(3)], axis=1).astype(BF16)
    for e, dq in enumerate((d0, d1, d2, d3)):
        total = None
        for d in range(4):
            one = mm(dq[(x + 4 - d) % 4], toks[d][...])
            total = one if total is None else total + one
        scr[(x + 4 - e) % 4] = total
    full = jnp.concatenate([scr[0], scr[1], scr[2], scr[3]], axis=0).T
    for r in range(4):
        rows[r] = full[96 * r : 96 * r + 96]
    c = c_ref[0]
    for h in range(2):
        keep_ref[h] = rows[2 * h + c]
        send_ref[h] = rows[2 * h + 1 - c].astype(BF16)


def term_q(xs, cs, toks, dqs, w_merge):
    return pl.pallas_call(
        term_q_kernel,
        in_specs=[smem()] * 2 + [vmem()] * 9,
        out_specs=[vmem()] * 4,
        out_shape=[
            jax.ShapeDtypeStruct((2, 96, HD), F32),
            jax.ShapeDtypeStruct((2, 96, HD), BF16),
            jax.ShapeDtypeStruct((3, 1024, 128), F32),
            jax.ShapeDtypeStruct((TOK, ROWS), BF16),
        ],
        scratch_shapes=[pltpu.VMEM((4, GROUP, ROWS), F32), pltpu.VMEM((4, 96, HD), F32)],
        compiler_params=params(12),
        cost_estimate=cost(4),
        name="term_q",
    )(xs, cs, *toks, *dqs, w_merge)


def natural(tiles, rows, put):
    left = lax.broadcasted_iota(jnp.int32, (rows, 128), 1) < 64
    for k in range(6):
        a = tiles(2 * k).astype(F32)
        b = tiles(2 * k + 1).astype(F32)
        put(128 * k, jnp.where(left, a, pltpu.roll(b, 64, 1)).astype(BF16))
        put(HD + 128 * k, jnp.where(left, pltpu.roll(a, 64, 1), b).astype(BF16))


def term_kv_kernel(x_ref, c_ref, tokf, merged_ref, k0, k1, k2, k3, wkv_ref, keep_ref, send_ref, tiles, dkv, full, m_ref):
    x = x_ref[0]
    c = c_ref[0]
    for e, k in enumerate((k0, k1, k2, k3)):
        group = (x + 4 - e) % 4
        for d in range(4):
            for h in range(3):
                tiles[group * 3 + h, pl.ds(64 * d, 64), :] = k[(x + 4 - d) % 4, h]

    def put(at, value):
        dkv[:, pl.ds(at, 128)] = value

    natural(lambda h: tiles[h], 256, put)
    grad = dkv[...]
    term = mm(merged_ref[...], grad, ((0,), (0,)))
    for r in range(4):
        full[r, :, pl.ds(0, D)] = term[96 * r : 96 * r + 96]
    dmerged = mm(grad, wkv_ref[...], ((1,), (1,)))
    for t in range(4):
        for k in range(3):
            one = dmerged[:, 128 * k : 128 * k + 128] * tokf[k, pl.ds(t, 256, stride=4), :]
            m_ref[t : t + 1, pl.ds(128 * k, 128)] = jnp.sum(one, axis=0, keepdims=True)
    m_ref[4:8, :] = jnp.zeros((4, ROWS), F32)
    m = m_ref[...]
    for r in range(4):
        full[r, :, pl.ds(D, 128)] = jnp.zeros((96, 128), F32)
        full[r, pl.ds(0, 8), pl.ds(D, 128)] = jnp.concatenate([m[:, 96 * r : 96 * r + 96], jnp.zeros((8, 32), F32)], axis=1)
    for h in range(2):
        keep_ref[h] = full[2 * h + c]
        send_ref[h] = full[2 * h + 1 - c].astype(BF16)


def term_kv(xs, cs, tokf, merged, dkvs, w_kv):
    spec = lambda shape: pl.BlockSpec(shape, lambda i, x, c: (0,) * len(shape))
    grid_spec = pltpu.PrefetchScalarGridSpec(
        num_scalar_prefetch=2,
        grid=(1,),
        in_specs=[spec((3, 1024, 128)), spec((TOK, ROWS))]
        + [spec((4, 3, CELLS, 128))] * 4
        + [spec((ROWS, D))],
        out_specs=[spec((2, 96, D + 128)), spec((2, 96, D + 128))],
        scratch_shapes=[
            pltpu.VMEM((12, 256, 128), BF16),
            pltpu.VMEM((256, D), BF16),
            pltpu.VMEM((4, 96, D + 128), F32),
            pltpu.VMEM((8, ROWS), F32),
        ],
    )
    return pl.pallas_call(
        term_kv_kernel,
        grid_spec=grid_spec,
        out_shape=[
            jax.ShapeDtypeStruct((2, 96, D + 128), F32),
            jax.ShapeDtypeStruct((2, 96, D + 128), BF16),
        ],
        compiler_params=params(11),
        cost_estimate=cost(5),
        name="term_kv",
    )(xs, cs, tokf, merged, *dkvs, w_kv)


def grad_tokens_kernel(x_ref, d0, d1, d2, d3, k0, k1, k2, k3, wq_ref, wkv_ref, wm_ref, out_ref, tiles, dkv, dqs, back):
    x = x_ref[0]
    for e, (q, k) in enumerate(((d0, k0), (d1, k1), (d2, k2), (d3, k3))):
        group = (x + 4 - e) % 4
        dqs[group] = q[0]
        for h in range(3):
            tiles[group * 3 + h] = k[0, h]

    def put(at, value):
        dkv[:, pl.ds(at, 128)] = value

    natural(lambda h: tiles[h], CELLS, put)
    dq = jnp.concatenate([dqs[g].astype(F32).T.astype(BF16) for g in range(4)], axis=1)
    full = mm(dq, wq_ref[...], ((1,), (1,)))
    dmerged = mm(dkv[...], wkv_ref[...], ((1,), (1,)))
    for k in range(12):
        lanes = pl.ds(128 * k, 128)
        back[k] = full[:, 128 * k : 128 * k + 128]
        for t in range(4):
            at = pl.ds(t, CELLS, stride=4)
            back[k, at, :] = back[k, at, :] + wm_ref[t : t + 1, lanes] * dmerged[:, 128 * k : 128 * k + 128]
        out_ref[0, :, lanes] = back[k].astype(BF16)


def grad_of_tokens(xs, dqs, dkvs, w_query, w_kv, w_merge):
    spec = lambda shape: pl.BlockSpec(shape, lambda i, x: (0,) * len(shape))
    grid_spec = pltpu.PrefetchScalarGridSpec(
        num_scalar_prefetch=1,
        grid=(1,),
        in_specs=[pl.BlockSpec((1, GROUP, TOK), lambda i, x: (x[0], 0, 0))] * 4
        + [pl.BlockSpec((1, 3, CELLS, 128), lambda i, x: (x[0], 0, 0, 0))] * 4
        + [spec((D, HD)), spec((D, D)), spec((4, D))],
        out_specs=spec((1, TOK, D)),
        scratch_shapes=[
            pltpu.VMEM((12, CELLS, 128), BF16),
            pltpu.VMEM((CELLS, D), BF16),
            pltpu.VMEM((4, GROUP, TOK), BF16),
            pltpu.VMEM((12, TOK, 128), F32),
        ],
    )
    return pl.pallas_call(
        grad_tokens_kernel,
        grid_spec=grid_spec,
        out_shape=jax.ShapeDtypeStruct((1, TOK, D), BF16),
        compiler_params=params(56),
        cost_estimate=cost(6),
        name="grad_tokens",
    )(xs, *dqs, *dkvs, w_query, w_kv, w_merge)


def spread_x(parts):
    return [parts[0]] + [lax.ppermute(parts[k], "seq", X_SHIFT[k]) for k in range(1, 4)]


def after(value, earlier):
    return lax.optimization_barrier((value, earlier))[0]


def core_sum(keep, send, y):
    got = lax.ppermute(send, "seq", CORE_SWAP)
    summed = keep + got.astype(F32)
    mine = lax.dynamic_index_in_dim(summed, y, 0, False)
    theirs = lax.dynamic_index_in_dim(summed, 1 - y, 0, False).astype(BF16)
    return mine, theirs


def on_device(tokens, keep_index, d_out, w_query, w_kv, w_merge):
    own = tokens[0]
    place = lax.axis_index("seq")
    x = place // 4
    y = (place // 2) % 2
    c = place % 2
    xs = x.reshape(1)
    cs = c.reshape(1)
    parts = keyval(xs, keep_index[0], own, w_merge, w_kv)
    got_kv = spread_x(parts)
    q_parts = queries(xs, keep_index, own, w_query, d_out[0])
    got_kv, q_parts = lax.optimization_barrier((got_kv, q_parts))
    unit = jnp.stack(got_kv)
    qs = spread_x(q_parts)
    unit_c = lax.ppermute(unit, "seq", CORE_SWAP)
    unit_y = lax.ppermute(unit, "seq", Y_SWAP)
    unit_cy = lax.ppermute(unit_y, "seq", CORE_SWAP)

    held = after(own, qs[1])
    slices = [lax.dynamic_slice(held, (0, ROWS * ((x + k) % 4)), (TOK, ROWS)) for k in range(4)]
    toks = spread_x(slices)

    a0, a1, a2, a3, dq, keep, send = attention(xs, qs, [unit, unit_y, unit_c, unit_cy])
    dq, keep, send, toks = lax.optimization_barrier((dq, keep, send, toks))
    dqs = [dq] + [lax.ppermute(dq, "seq", X_SHIFT[k]) for k in range(1, 4)]
    core = lax.ppermute(send, "seq", CORE_SWAP)
    other = (keep[:, 256:] + core[:, 256:].astype(F32)).astype(BF16)
    from_y = lax.ppermute(other, "seq", Y_SWAP)
    taps, weights = after((w_merge, w_kv), other)
    taps = lax.dynamic_slice(taps, (0, ROWS * x), (4, ROWS))
    weights = lax.dynamic_slice(weights, (ROWS * x, 0), (ROWS, D))
    tables = key_tables(after(qs, other))
    dkv = finish_dkv(xs, tables, keep, core, from_y)
    dkvs = [dkv] + [lax.ppermute(dkv, "seq", X_SHIFT[k]) for k in range(1, 4)]

    keep_q, send_q, tokf, unit_merged = term_q(xs, cs, toks, after(dqs, dkv), taps)
    keep_kv, send_kv = term_kv(xs, cs, tokf, unit_merged, dkvs, weights)
    mine_q, theirs_q = core_sum(keep_q, after(send_q, dkv), y)

    mine, theirs = core_sum(keep_kv, send_kv, y)
    theirs_q = after(theirs_q, theirs)
    got_q = lax.ppermute(theirs_q, "seq", Y_SWAP)
    got = lax.ppermute(theirs, "seq", Y_SWAP)
    grads = grad_of_tokens(xs, after(dqs, (theirs, theirs_q)), dkvs, w_query, w_kv, w_merge)
    got, got_q = after((got, got_q), grads)
    total = mine + got.astype(F32)
    total = total.astype(BF16)
    m = jnp.broadcast_to(total[None, :24, D:], (8, 24, 128))
    total = total[:, :D].reshape(4, 24, 2, 768).transpose(0, 2, 1, 3).reshape(8, 24, 768)
    total_q = (mine_q + got_q.astype(F32)).astype(BF16)
    total_q = total_q.reshape(4, 24, 2, 384).transpose(0, 2, 1, 3).reshape(8, 24, 384)
    chunks = jnp.concatenate([total_q, total, m], axis=2)
    shards = lax.all_to_all(chunks, "dp", 0, 0, axis_index_groups=Z_GROUPS)
    a1, a2, a3 = after((a1, a2, a3), chunks)
    back = [a0] + [lax.ppermute(a, "seq", X_SHIFT[4 - k]) for k, a in ((1, a1), (2, a2), (3, a3))]
    order = jnp.stack(back)
    att = jnp.concatenate([lax.dynamic_index_in_dim(order, (g + 4 - x) % 4, 0, False) for g in range(4)], axis=0)
    attended = att.T

    shard = jnp.sum(shards.astype(F32), axis=0).astype(BF16)
    pair = lax.ppermute(shard, "dp", YLO_SWAP)
    shard = shard.astype(F32) + pair.astype(F32)
    grad_m = shard[:4, 1152 : 1152 + 96]
    final = shard[:, :1152].astype(BF16)
    final = lax.all_to_all(jnp.broadcast_to(final[None], (8, 24, 1152)), "dp", 0, 0, axis_index_groups=Z_GROUPS)
    final = final.reshape(4, 2, 24, 1152).transpose(0, 2, 1, 3)
    grad_q = final[..., :384].reshape(96, HD).astype(F32)
    grad_kv = final[..., 384:].reshape(96, D).astype(F32)
    return attended[None], grads, grad_q, grad_kv, grad_m


def solution(mesh):
    placed = (P("dp", "seq", None), P("dp", "seq"), P("dp", "seq", None), P(), P(), P())
    return jax.shard_map(
        on_device,
        mesh=mesh,
        in_specs=placed,
        out_specs=(
            P("dp", "seq", None),
            P("dp", "seq", None),
            P("seq", None),
            P("seq", None),
            P(None, "seq"),
        ),
        check_vma=False,
    )
```

profile of v0, /device:TPU:2, one launch (start us, length us, event | category | flops | bytes accessed | tf_op | source)
XLA Modules:
  0.0 149.3 jit_solution(15642842502127558050)
XLA Ops:
  0.7 4.8 %keyval.1 = (bf16[3,64,128]{2,1,0:T(8,128)(2,1)}, bf16[3,64,128]{2,1,0:T(8,128)(2,1)}, bf16[3,64,128]{2,1,0:T(8,128)(2,1)}, bf16[3,64,128]{2,1,0:T(8,128)(2,1)}) custom-call(s32[1]{0:T(128)} %bitcast.x_ref, s32[256]{0:T(256)} %bitcast.56, bf16[256,1536]{1,0:T(8,128)(2,1)} %bitcast.52, f32[4,1536]{1,0:T(4,128)} %wm_ref.1, bf16[1536,1536]{1,0:T(8,128)(2,1)} %wkv_ref.3), custom_call_target="tpu_custom_call" | custom-call | flops 6600000000 | bytes 600000 | tf_op jit(solution)/shard_map/keyval/pallas_call | solution.py:119
  5.5 1.6 %collective-permute-start = (bf16[3,64,128]{2,1,0:T(8,128)(2,1)}, bf16[3,64,128]{2,1,0:T(8,128)(2,1)S(1)}, u32[]{:S(2)}, u32[]{:S(2)}) collective-permute-start(bf16[3,64,128]{2,1,0:T(8,128)(2,1)} %get-tuple-element.66), channel_id=1, source_target_pairs={{0,4},{1,5},{2,6},{3,7},{4,8},{5,9},{6,10},{7,11},{8,12},{9,13},{1... | collective-permute-start | bytes 147464 | tf_op jit(solution)/shard_map/ppermute | solution.py:499
  7.1 2.8 %collective-permute-start.1 = (bf16[3,64,128]{2,1,0:T(8,128)(2,1)}, bf16[3,64,128]{2,1,0:T(8,128)(2,1)S(1)}, u32[]{:S(2)}, u32[]{:S(2)}) collective-permute-start(bf16[3,64,128]{2,1,0:T(8,128)(2,1)} %get-tuple-element.67), channel_id=1, source_target_pairs={{0,8},{1,9},{2,10},{3,11},{4,12},{5,13},{6,14},{7,15},{8,0},{9,1},... | collective-permute-start | bytes 147464 | tf_op jit(solution)/shard_map/ppermute | solution.py:499
  10.0 0.4 collective-permute-start.2
  10.4 1.0 queries.1
  11.5 1.5 collective-permute-done.1
  12.9 1.3 collective-permute-done.2
  14.3 2.1 %collective-permute-start.6 = (bf16[4,3,64,128]{3,2,1,0:T(8,128)(2,1)S(1)}, bf16[4,3,64,128]{3,2,1,0:T(8,128)(2,1)S(1)}, u32[]{:S(2)}, u32[]{:S(2)}) collective-permute-start(bf16[4,3,64,128]{3,2,1,0:T(8,128)(2,1)S(1)} %pad_maximum_fusion.2.u0), channel_id=1, source_target_pairs={{0,2},{1,3},{2,0},{3,1},{4,6},{5,7},{6,4},{7,5},{8,10},{9,11},{10,... | collective-permute-start | bytes 589832 | tf_op jit(solution)/shard_map/ppermute | solution.py:529
  16.4 1.1 collective-permute-start.3
  17.4 2.6 %collective-permute-start.4 = (bf16[400,256]{1,0:T(8,128)(2,1)S(1)}, bf16[400,256]{1,0:T(8,128)(2,1)S(1)}, u32[]{:S(2)}, u32[]{:S(2)}) collective-permute-start(bf16[400,256]{1,0:T(8,128)(2,1)S(1)} %get-tuple-element.75), channel_id=1, source_target_pairs={{0,8},{1,9},{2,10},{3,11},{4,12},{5,13},{6,14},{7,15},{8,0},{9,1},... | collective-permute-start | bytes 614408 | tf_op jit(solution)/shard_map/ppermute | solution.py:499
  20.1 2.0 %collective-permute-start.5 = (bf16[400,256]{1,0:T(8,128)(2,1)S(1)}, bf16[400,256]{1,0:T(8,128)(2,1)S(1)}, u32[]{:S(2)}, u32[]{:S(2)}) collective-permute-start(bf16[400,256]{1,0:T(8,128)(2,1)S(1)} %get-tuple-element.76), channel_id=1, source_target_pairs={{0,12},{1,13},{2,14},{3,15},{4,0},{5,1},{6,2},{7,3},{8,4},{9,5},{1... | collective-permute-start | bytes 614408 | tf_op jit(solution)/shard_map/ppermute | solution.py:499
  22.1 0.5 collective-permute-start.8
  22.6 1.4 collective-permute-done.3.q1
  24.1 2.7 %collective-permute-start.10 = (bf16[256,384]{1,0:T(8,128)(2,1)S(1)}, bf16[256,384]{1,0:T(8,128)(2,1)S(1)}, u32[]{:S(2)}, u32[]{:S(2)}) collective-permute-start(bf16[256,384]{1,0:T(8,128)(2,1)S(1)} %get-tuple-element.136), channel_id=1, source_target_pairs={{0,8},{1,9},{2,10},{3,11},{4,12},{5,13},{6,14},{7,15},{8,0},{9,1},... | collective-permute-start | bytes 589832 | tf_op jit(solution)/shard_map/ppermute | solution.py:499
  26.9 0.6 collective-permute-start.11
  27.5 1.7 %collective-permute-start.9 = (bf16[256,384]{1,0:T(8,128)(2,1)S(1)}, bf16[256,384]{1,0:T(8,128)(2,1)S(1)}, u32[]{:S(2)}, u32[]{:S(2)}) collective-permute-start(bf16[256,384]{1,0:T(8,128)(2,1)S(1)} %get-tuple-element.137), channel_id=1, source_target_pairs={{0,4},{1,5},{2,6},{3,7},{4,8},{5,9},{6,10},{7,11},{8,12},{9,13},{1... | collective-permute-start | bytes 589832 | tf_op jit(solution)/shard_map/ppermute | solution.py:499
  29.2 4.7 %collective-permute-done.5.q3 = bf16[400,256]{1,0:T(8,128)(2,1)S(1)} collective-permute-done((bf16[400,256]{1,0:T(8,128)(2,1)S(1)}, bf16[400,256]{1,0:T(8,128)(2,1)S(1)}, u32[]{:S(2)}, u32[]{:S(2)}) %collective-permute-start.5) | collective-permute-done | bytes 204832 | tf_op jit(solution)/shard_map/ppermute | solution.py:499
  33.9 0.6 copy-done.19
  34.6 0.7 copy-done.22
  35.2 17.6 %attention.1 = (bf16[192,256]{1,0:T(8,128)(2,1)}, bf16[192,256]{1,0:T(8,128)(2,1)}, bf16[192,256]{1,0:T(8,128)(2,1)}, bf16[192,256]{1,0:T(8,128)(2,1)}, bf16[4,1...) custom-call(s32[1]{0:T(128)} %bitcast.x_ref, bf16[400,256]{1,0:T(8,128)(2,1)} %copy-done.12, ...), custom_call_target="tpu_custom_call" | custom-call | flops 22000001024 | bytes 2000000 | tf_op jit(solution)/shard_map/attention/pallas_call | solution.py:263
  52.8 0.1 collective-permute-start.15
  53.0 1.3 collective-permute-start.13
  54.3 2.5 %collective-permute-start.14 = (bf16[4,192,256]{2,1,0:T(8,128)(2,1)}, bf16[4,192,256]{2,1,0:T(8,128)(2,1)S(1)}, u32[]{:S(2)}, u32[]{:S(2)}) collective-permute-start(bf16[4,192,256]{2,1,0:T(8,128)(2,1)} %get-tuple-element.116.d0), channel_id=1, source_target_pairs={{0,12},{1,13},{2,14},{3,15},{4,0},{5,1},{6,2},{7,3},{8,4},{9,5},{1... | collective-permute-start | bytes 1179656 | tf_op jit(solution)/shard_map/ppermute | solution.py:538
  56.8 1.2 add_convert_fusion
  58.0 0.1 collective-permute-start.16
  58.1 0.7 constant_dynamic-slice_fusion.1.wm_ref
  58.8 1.3 constant_dynamic-slice_fusion.wkv_ref
  60.2 2.5 %key_tables.1 = (f32[256,128]{1,0:T(8,128)}, f32[256,128]{1,0:T(8,128)}) custom-call(bf16[400,256]{1,0:T(8,128)(2,1)} %copy-done.12, bf16[400,256]{1,0:T(8,128)(2,1)} %copy-done.17, bf16[400,256]{1,0:T(8,128)(2,1)} %copy-done.18, bf16[400,256]{1,0:T(8,128)(2,1)} %copy-done.19), custom_call_target="tpu_custom_call" | custom-call | flops 2200000000 | bytes 200000 | tf_op jit(solution)/shard_map/key_tables/pallas_call | solution.py:303
  62.6 3.4 %collective-permute-done.16.y_ref = bf16[3,256,128]{2,1,0:T(8,128)(2,1)S(1)} collective-permute-done((bf16[3,256,128]{2,1,0:T(8,128)(2,1)S(1)}, bf16[3,256,128]{2,1,0:T(8,128)(2,1)S(1)}, u32[]{:S(2)}, u32[]{:S(2)}) %collective-permute-start.16) | collective-permute-done | bytes 196640 | tf_op jit(solution)/shard_map/ppermute | solution.py:541
  66.0 0.7 copy-done.23
  66.7 2.2 %finish_dkv.1.k0 = bf16[4,3,64,128]{3,2,1,0:T(8,128)(2,1)} custom-call(s32[1]{0:T(128)} %bitcast.x_ref, f32[256,128]{1,0:T(8,128)} %get-tuple-element.100.cos_ref, f32[256,128]{1,0:T(8,128)} %get-tuple-element.101.sin_ref, f32[3,512,128]{2,1,0:T(8,128)} %get-tuple-element.94.keep_ref, bf16[3,512,128]{2,1,0:T(8,128)(2,1)} %copy-done.15, ...), custom_call_target="tpu_custom_call" | custom-call | flops 2200000000 | bytes 200000 | tf_op jit(solution)/shard_map/finish_dkv/pallas_call | solution.py:326
  68.9 3.2 %collective-permute-start.19 = (bf16[4,3,64,128]{3,2,1,0:T(8,128)(2,1)}, bf16[4,3,64,128]{3,2,1,0:T(8,128)(2,1)S(1)}, u32[]{:S(2)}, u32[]{:S(2)}) collective-permute-start(bf16[4,3,64,128]{3,2,1,0:T(8,128)(2,1)} %finish_dkv.1.k0), channel_id=1, source_target_pairs={{0,8},{1,9},{2,10},{3,11},{4,12},{5,13},{6,14},{7,15},{8,0},{9,1},... | collective-permute-start | bytes 589832 | tf_op jit(solution)/shard_map/ppermute | solution.py:547
  72.1 0.6 collective-permute-start.20
  72.7 2.6 %collective-permute-done.14.d3 = bf16[4,192,256]{2,1,0:T(8,128)(2,1)S(1)} collective-permute-done((bf16[4,192,256]{2,1,0:T(8,128)(2,1)}, bf16[4,192,256]{2,1,0:T(8,128)(2,1)S(1)}, u32[]{:S(2)}, u32[]{:S(2)}) %collective-permute-start.14) | collective-permute-done | bytes 393248 | tf_op jit(solution)/shard_map/ppermute | solution.py:538
  75.3 2.4 %term_q.1 = (f32[2,96,768]{2,1,0:T(8,128)S(1)}, bf16[2,96,768]{2,1,0:T(8,128)(2,1)}, f32[3,1024,128]{2,1,0:T(8,128)S(1)}, bf16[256,384]{1,0:T(8,128)(2,1)S(1)}) custom-call(s32[1]{0:T(128)} %bitcast.x_ref, s32[1]{0:T(128)} %bitcast.9.c_ref, bf16[256,384]{1,0:T(8,128)(2,1)S(1)} %get-tuple-element.89.t0, bf16[256,384]{1,0:T(8,128)(2,1)S(1)} %collective-permute-done.9.t1, ...), custom_call_target="tpu_custom_call" | custom-call | flops 4400000000 | bytes 400000 | tf_op jit(solution)/shard_map/term_q/pallas_call | solution.py:361
  77.7 0.1 collective-permute-start.17
  77.8 1.7 %collective-permute-done.19.k2 = bf16[4,3,64,128]{3,2,1,0:T(8,128)(2,1)S(1)} collective-permute-done((bf16[4,3,64,128]{3,2,1,0:T(8,128)(2,1)}, bf16[4,3,64,128]{3,2,1,0:T(8,128)(2,1)S(1)}, u32[]{:S(2)}, u32[]{:S(2)}) %collective-permute-start.19) | collective-permute-done | bytes 196640 | tf_op jit(solution)/shard_map/ppermute | solution.py:547
  79.5 3.2 %collective-permute-done.20.k3 = bf16[4,3,64,128]{3,2,1,0:T(8,128)(2,1)S(1)} collective-permute-done((bf16[4,3,64,128]{3,2,1,0:T(8,128)(2,1)}, bf16[4,3,64,128]{3,2,1,0:T(8,128)(2,1)S(1)}, u32[]{:S(2)}, u32[]{:S(2)}) %collective-permute-start.20) | collective-permute-done | bytes 196640 | tf_op jit(solution)/shard_map/ppermute | solution.py:547
  82.7 1.5 term_kv.1
  84.2 0.1 collective-permute-start.21
  84.5 1.9 %collective-permute-done.21 = bf16[2,96,1664]{2,1,0:T(8,128)(2,1)S(1)} collective-permute-done((bf16[2,96,1664]{2,1,0:T(8,128)(2,1)S(1)}, bf16[2,96,1664]{2,1,0:T(8,128)(2,1)S(1)}, u32[]{:S(2)}, u32[]{:S(2)}) %collective-permute-start.21) | collective-permute-done | bytes 639008 | tf_op jit(solution)/shard_map/ppermute | solution.py:507
  86.4 0.1 convert_add_fusion
  86.6 0.1 collective-permute-start.22
  86.7 3.5 %collective-permute-start.23 = (bf16[96,768]{1,0:T(8,128)(2,1)S(1)}, bf16[96,768]{1,0:T(8,128)(2,1)S(1)}, u32[]{:S(2)}, u32[]{:S(2)}) collective-permute-start(bf16[96,768]{1,0:T(8,128)(2,1)S(1)} %fusion.3), channel_id=1, source_target_pairs={{0,2},{1,3},{2,0},{3,1},{4,6},{5,7},{6,4},{7,5},{8,10},{9,11},{10,... | collective-permute-start | bytes 442376 | tf_op jit(solution)/shard_map/ppermute | solution.py:555
  90.2 6.8 %grad_tokens.1 = bf16[1,256,1536]{2,1,0:T(8,128)(2,1)} custom-call(s32[1]{0:T(128)} %bitcast.x_ref, bf16[4,192,256]{2,1,0:T(8,128)(2,1)} %get-tuple-element.116.d0, bf16[4,192,256]{2,1,0:T(8,128)(2,1)} %copy-done.4, bf16[4,192,256]{2,1,0:T(8,128)(2,1)} %copy-done.5, bf16[4,192,256]{2,1,0:T(8,128)(2,1)} %copy-done.6, bf16[4,3,64,128]{3,2,1,0:T(8,128)(2,1)} %finish_dkv.1.k0, ...), custom_call_target="tpu_custom_call" | custom-call | flops 6600000000 | bytes 600000 | tf_op jit(solution)/shard_map/grad_tokens/pallas_call | solution.py:488
  97.0 3.9 %collective-permute-done.23 = bf16[96,768]{1,0:T(8,128)(2,1)S(1)} collective-permute-done((bf16[96,768]{1,0:T(8,128)(2,1)S(1)}, bf16[96,768]{1,0:T(8,128)(2,1)S(1)}, u32[]{:S(2)}, u32[]{:S(2)}) %collective-permute-start.23) | collective-permute-done | bytes 147488 | tf_op jit(solution)/shard_map/ppermute | solution.py:555
  101.3 24.6 %all_to_all.10 = bf16[8,24,1280]{2,1,0:T(8,128)(2,1)S(1)} all-to-all(bf16[8,24,1280]{2,1,0:T(8,128)(2,1)S(1)} %pad_maximum_fusion), channel_id=1, replica_groups={{0,16,32,48,64,80,96,112},{128,144,160,176,192,208,224,240},{1,17,33,49..., dimensions={0} | all-to-all | bytes 983040 | tf_op jit(solution)/shard_map/all_to_all | solution.py:566
  126.0 0.1 collective-permute-start.27
  126.1 4.2 %collective-permute-done.27 = bf16[24,1280]{1,0:T(8,128)(2,1)S(1)} collective-permute-done((bf16[24,1280]{1,0:T(8,128)(2,1)S(1)}, bf16[24,1280]{1,0:T(8,128)(2,1)S(1)}, u32[]{:S(2)}, u32[]{:S(2)}) %collective-permute-start.27) | collective-permute-done | bytes 61472 | tf_op jit(solution)/shard_map/ppermute | solution.py:574
  130.3 0.8 broadcast_in_dim.8
  131.1 3.5 %all-to-all-start.1 = ((bf16[8,24,1152]{2,1,0:T(8,128)(2,1)}), bf16[8,24,1152]{2,1,0:T(8,128)(2,1)S(1)}, u32[]{:S(2)}, u32[]{:S(2)}) async-start(bf16[8,24,1152]{2,1,0:T(8,128)(2,1)} %broadcast_in_dim.8), calls=%async_computation.1 | async-start | bytes 884736 | tf_op jit(solution)/shard_map/all_to_all | solution.py:578
  134.6 0.4 collective-permute-start.24
  135.1 2.0 %collective-permute-start.25 = (bf16[192,256]{1,0:T(8,128)(2,1)S(1)}, bf16[192,256]{1,0:T(8,128)(2,1)S(1)}, u32[]{:S(2)}, u32[]{:S(2)}) collective-permute-start(bf16[192,256]{1,0:T(8,128)(2,1)S(1)} %copy-done.25), channel_id=1, source_target_pairs={{0,8},{1,9},{2,10},{3,11},{4,12},{5,13},{6,14},{7,15},{8,0},{9,1},... | collective-permute-start | bytes 294920 | tf_op jit(solution)/shard_map/ppermute | solution.py:568
  137.1 1.5 collective-permute-start.26
  138.6 0.8 collective-permute-done.24
  139.3 1.9 %collective-permute-done.25 = bf16[192,256]{1,0:T(8,128)(2,1)S(1)} collective-permute-done((bf16[192,256]{1,0:T(8,128)(2,1)S(1)}, bf16[192,256]{1,0:T(8,128)(2,1)S(1)}, u32[]{:S(2)}, u32[]{:S(2)}) %collective-permute-start.25) | collective-permute-done | bytes 98336 | tf_op jit(solution)/shard_map/ppermute | solution.py:568
  141.2 1.2 collective-permute-done.26
  142.6 0.9 copy.18
  143.5 0.6 slice.39
  144.1 3.1 %all-to-all-done.1 = bf16[8,24,1152]{2,1,0:T(8,128)(2,1)S(1)} async-done(((bf16[8,24,1152]{2,1,0:T(8,128)(2,1)}), bf16[8,24,1152]{2,1,0:T(8,128)(2,1)S(1)}, u32[]{:S(2)}, u32[]{:S(2)}) %all-to-all-start.1) | async-done | bytes 442400 | tf_op jit(solution)/shard_map/all_to_all | solution.py:578
  147.2 0.3 copy.17
  147.5 0.9 copy.20
  148.4 0.2 copy.16
  148.6 0.7 copy.19
  (91 shorter events, 1.1 us)
Async XLA Ops:
  0.6 9.7 %copy-start = (bf16[1,256,1536]{2,1,0:T(8,128)(2,1)S(1)}, bf16[1,256,1536]{2,1,0:T(8,128)(2,1)}, u32[]{:S(2)}) copy-start(bf16[1,256,1536]{2,1,0:T(8,128)(2,1)} %param.6) | copy-start | bytes 2359300
  0.7 9.7 %copy-start.1 = (bf16[1536,768]{1,0:T(8,128)(2,1)S(1)}, bf16[1536,768]{1,0:T(8,128)(2,1)}, u32[]{:S(2)}) copy-start(bf16[1536,768]{1,0:T(8,128)(2,1)} %wq_ref.3) | copy-start | bytes 7077892
  0.7 9.7 %copy-start.2 = (bf16[1,256,768]{2,1,0:T(8,128)(2,1)S(1)}, bf16[1,256,768]{2,1,0:T(8,128)(2,1)}, u32[]{:S(2)}) copy-start(bf16[1,256,768]{2,1,0:T(8,128)(2,1)} %param.8) | copy-start | bytes 1179652
  0.7 9.7 %copy-start.11 = (s32[1,256]{1,0:T(1,128)S(1)}, s32[1,256]{1,0:T(1,128)}, u32[]{:S(2)}) copy-start(s32[1,256]{1,0:T(1,128)} %idx_ref.1) | copy-start | bytes 3076
  5.5 5.9 %collective-permute-start = (bf16[3,64,128]{2,1,0:T(8,128)(2,1)}, bf16[3,64,128]{2,1,0:T(8,128)(2,1)S(1)}, u32[]{:S(2)}, u32[]{:S(2)}) collective-permute-start(bf16[3,64,128]{2,1,0:T(8,128)(2,1)} %get-tuple-element.66), channel_id=1, source_target_pairs={{0,4},{1,5},{2,6},{3,7},{4,8},{5,9},{6,10},{7,11},{8,12},{9,13},{1... | collective-permute-start | bytes 147464 | tf_op jit(solution)/shard_map/ppermute | solution.py:499
  7.1 5.8 %collective-permute-start.1 = (bf16[3,64,128]{2,1,0:T(8,128)(2,1)}, bf16[3,64,128]{2,1,0:T(8,128)(2,1)S(1)}, u32[]{:S(2)}, u32[]{:S(2)}) collective-permute-start(bf16[3,64,128]{2,1,0:T(8,128)(2,1)} %get-tuple-element.67), channel_id=1, source_target_pairs={{0,8},{1,9},{2,10},{3,11},{4,12},{5,13},{6,14},{7,15},{8,0},{9,1},... | collective-permute-start | bytes 147464 | tf_op jit(solution)/shard_map/ppermute | solution.py:499
  10.0 4.3 %collective-permute-start.2 = (bf16[3,64,128]{2,1,0:T(8,128)(2,1)}, bf16[3,64,128]{2,1,0:T(8,128)(2,1)S(1)}, u32[]{:S(2)}, u32[]{:S(2)}) collective-permute-start(bf16[3,64,128]{2,1,0:T(8,128)(2,1)} %get-tuple-element.68), channel_id=1, source_target_pairs={{0,12},{1,13},{2,14},{3,15},{4,0},{5,1},{6,2},{7,3},{8,4},{9,5},{1... | collective-permute-start | bytes 147464 | tf_op jit(solution)/shard_map/ppermute | solution.py:499
  10.4 3.9 %copy-start.16 = (bf16[3,64,128]{2,1,0:T(8,128)(2,1)S(1)}, bf16[3,64,128]{2,1,0:T(8,128)(2,1)}, u32[]{:S(2)}) copy-start(bf16[3,64,128]{2,1,0:T(8,128)(2,1)} %get-tuple-element.77) | copy-start | bytes 147460
  11.4 10.7 %copy-start.12 = (bf16[400,256]{1,0:T(8,128)(2,1)}, bf16[400,256]{1,0:T(8,128)(2,1)S(1)}, u32[]{:S(2)}) copy-start(bf16[400,256]{1,0:T(8,128)(2,1)S(1)} %get-tuple-element.96.q0) | copy-start | bytes 614404
  14.3 19.6 %copy-start.13 = (bf16[4,3,64,128]{3,2,1,0:T(8,128)(2,1)}, bf16[4,3,64,128]{3,2,1,0:T(8,128)(2,1)S(1)}, u32[]{:S(2)}) copy-start(bf16[4,3,64,128]{3,2,1,0:T(8,128)(2,1)S(1)} %pad_maximum_fusion.2.u0) | copy-start | bytes 589828
  14.3 7.8 %collective-permute-start.6 = (bf16[4,3,64,128]{3,2,1,0:T(8,128)(2,1)S(1)}, bf16[4,3,64,128]{3,2,1,0:T(8,128)(2,1)S(1)}, u32[]{:S(2)}, u32[]{:S(2)}) collective-permute-start(bf16[4,3,64,128]{3,2,1,0:T(8,128)(2,1)S(1)} %pad_maximum_fusion.2.u0), channel_id=1, source_target_pairs={{0,2},{1,3},{2,0},{3,1},{4,6},{5,7},{6,4},{7,5},{8,10},{9,11},{10,... | collective-permute-start | bytes 589832 | tf_op jit(solution)/shard_map/ppermute | solution.py:529
  16.4 7.6 %collective-permute-start.3 = (bf16[400,256]{1,0:T(8,128)(2,1)S(1)}, bf16[400,256]{1,0:T(8,128)(2,1)S(1)}, u32[]{:S(2)}, u32[]{:S(2)}) collective-permute-start(bf16[400,256]{1,0:T(8,128)(2,1)S(1)} %get-tuple-element.74), channel_id=1, source_target_pairs={{0,4},{1,5},{2,6},{3,7},{4,8},{5,9},{6,10},{7,11},{8,12},{9,13},{1... | collective-permute-start | bytes 614408 | tf_op jit(solution)/shard_map/ppermute | solution.py:499
  17.4 10.0 %collective-permute-start.4 = (bf16[400,256]{1,0:T(8,128)(2,1)S(1)}, bf16[400,256]{1,0:T(8,128)(2,1)S(1)}, u32[]{:S(2)}, u32[]{:S(2)}) collective-permute-start(bf16[400,256]{1,0:T(8,128)(2,1)S(1)} %get-tuple-element.75), channel_id=1, source_target_pairs={{0,8},{1,9},{2,10},{3,11},{4,12},{5,13},{6,14},{7,15},{8,0},{9,1},... | collective-permute-start | bytes 614408 | tf_op jit(solution)/shard_map/ppermute | solution.py:499
  20.1 13.8 %collective-permute-start.5 = (bf16[400,256]{1,0:T(8,128)(2,1)S(1)}, bf16[400,256]{1,0:T(8,128)(2,1)S(1)}, u32[]{:S(2)}, u32[]{:S(2)}) collective-permute-start(bf16[400,256]{1,0:T(8,128)(2,1)S(1)} %get-tuple-element.76), channel_id=1, source_target_pairs={{0,12},{1,13},{2,14},{3,15},{4,0},{5,1},{6,2},{7,3},{8,4},{9,5},{1... | collective-permute-start | bytes 614408 | tf_op jit(solution)/shard_map/ppermute | solution.py:499
  22.1 4.7 %collective-permute-start.7 = (bf16[4,3,64,128]{3,2,1,0:T(8,128)(2,1)S(1)}, bf16[4,3,64,128]{3,2,1,0:T(8,128)(2,1)S(1)}, u32[]{:S(2)}, u32[]{:S(2)}) collective-permute-start(bf16[4,3,64,128]{3,2,1,0:T(8,128)(2,1)S(1)} %pad_maximum_fusion.2.u0), channel_id=1, source_target_pairs={{0,1},{1,0},{2,3},{3,2},{4,5},{5,4},{6,7},{7,6},{8,9},{9,8},{10,11... | collective-permute-start | bytes 589832 | tf_op jit(solution)/shard_map/ppermute | solution.py:528
  22.1 11.8 %copy-start.20 = (bf16[4,3,64,128]{3,2,1,0:T(8,128)(2,1)}, bf16[4,3,64,128]{3,2,1,0:T(8,128)(2,1)S(1)}, u32[]{:S(2)}) copy-start(bf16[4,3,64,128]{3,2,1,0:T(8,128)(2,1)S(1)} %collective-permute-done.6.u1) | copy-start | bytes 589828
  22.1 11.7 %collective-permute-start.8 = (bf16[4,3,64,128]{3,2,1,0:T(8,128)(2,1)S(1)}, bf16[4,3,64,128]{3,2,1,0:T(8,128)(2,1)S(1)}, u32[]{:S(2)}, u32[]{:S(2)}) collective-permute-start(bf16[4,3,64,128]{3,2,1,0:T(8,128)(2,1)S(1)} %collective-permute-done.6.u1), channel_id=1, source_target_pairs={{0,1},{1,0},{2,3},{3,2},{4,5},{5,4},{6,7},{7,6},{8,9},{9,8},{10,11... | collective-permute-start | bytes 589832 | tf_op jit(solution)/shard_map/ppermute | solution.py:530
  24.0 9.9 %copy-start.17 = (bf16[400,256]{1,0:T(8,128)(2,1)}, bf16[400,256]{1,0:T(8,128)(2,1)S(1)}, u32[]{:S(2)}) copy-start(bf16[400,256]{1,0:T(8,128)(2,1)S(1)} %collective-permute-done.3.q1) | copy-start | bytes 614404
  24.1 28.7 %collective-permute-start.10 = (bf16[256,384]{1,0:T(8,128)(2,1)S(1)}, bf16[256,384]{1,0:T(8,128)(2,1)S(1)}, u32[]{:S(2)}, u32[]{:S(2)}) collective-permute-start(bf16[256,384]{1,0:T(8,128)(2,1)S(1)} %get-tuple-element.136), channel_id=1, source_target_pairs={{0,8},{1,9},{2,10},{3,11},{4,12},{5,13},{6,14},{7,15},{8,0},{9,1},... | collective-permute-start | bytes 589832 | tf_op jit(solution)/shard_map/ppermute | solution.py:499
  26.9 7.1 %copy-start.21 = (bf16[4,3,64,128]{3,2,1,0:T(8,128)(2,1)}, bf16[4,3,64,128]{3,2,1,0:T(8,128)(2,1)S(1)}, u32[]{:S(2)}) copy-start(bf16[4,3,64,128]{3,2,1,0:T(8,128)(2,1)S(1)} %collective-permute-done.7.u2) | copy-start | bytes 589828
  26.9 25.9 %collective-permute-start.11 = (bf16[256,384]{1,0:T(8,128)(2,1)S(1)}, bf16[256,384]{1,0:T(8,128)(2,1)S(1)}, u32[]{:S(2)}, u32[]{:S(2)}) collective-permute-start(bf16[256,384]{1,0:T(8,128)(2,1)S(1)} %get-tuple-element.135), channel_id=1, source_target_pairs={{0,12},{1,13},{2,14},{3,15},{4,0},{5,1},{6,2},{7,3},{8,4},{9,5},{1... | collective-permute-start | bytes 589832 | tf_op jit(solution)/shard_map/ppermute | solution.py:499
  27.5 6.4 %copy-start.18 = (bf16[400,256]{1,0:T(8,128)(2,1)}, bf16[400,256]{1,0:T(8,128)(2,1)S(1)}, u32[]{:S(2)}) copy-start(bf16[400,256]{1,0:T(8,128)(2,1)S(1)} %collective-permute-done.4.q2) | copy-start | bytes 614404
  27.5 25.3 %collective-permute-start.9 = (bf16[256,384]{1,0:T(8,128)(2,1)S(1)}, bf16[256,384]{1,0:T(8,128)(2,1)S(1)}, u32[]{:S(2)}, u32[]{:S(2)}) collective-permute-start(bf16[256,384]{1,0:T(8,128)(2,1)S(1)} %get-tuple-element.137), channel_id=1, source_target_pairs={{0,4},{1,5},{2,6},{3,7},{4,8},{5,9},{6,10},{7,11},{8,12},{9,13},{1... | collective-permute-start | bytes 589832 | tf_op jit(solution)/shard_map/ppermute | solution.py:499
  33.9 0.7 copy-start.19
  34.6 0.7 copy-start.22
  52.8 4.0 %collective-permute-start.15 = (bf16[3,512,128]{2,1,0:T(8,128)(2,1)}, bf16[3,512,128]{2,1,0:T(8,128)(2,1)S(1)}, u32[]{:S(2)}, u32[]{:S(2)}) collective-permute-start(bf16[3,512,128]{2,1,0:T(8,128)(2,1)} %get-tuple-element.95), channel_id=1, source_target_pairs={{0,1},{1,0},{2,3},{3,2},{4,5},{5,4},{6,7},{7,6},{8,9},{9,8},{10,11... | collective-permute-start | bytes 1179656 | tf_op jit(solution)/shard_map/ppermute | solution.py:539
  52.9 19.2 %collective-permute-start.12 = (bf16[4,192,256]{2,1,0:T(8,128)(2,1)}, bf16[4,192,256]{2,1,0:T(8,128)(2,1)S(1)}, u32[]{:S(2)}, u32[]{:S(2)}) collective-permute-start(bf16[4,192,256]{2,1,0:T(8,128)(2,1)} %get-tuple-element.116.d0), channel_id=1, source_target_pairs={{0,4},{1,5},{2,6},{3,7},{4,8},{5,9},{6,10},{7,11},{8,12},{9,13},{1... | collective-permute-start | bytes 1179656 | tf_op jit(solution)/shard_map/ppermute | solution.py:538
  53.0 19.7 %collective-permute-start.13 = (bf16[4,192,256]{2,1,0:T(8,128)(2,1)}, bf16[4,192,256]{2,1,0:T(8,128)(2,1)S(1)}, u32[]{:S(2)}, u32[]{:S(2)}) collective-permute-start(bf16[4,192,256]{2,1,0:T(8,128)(2,1)} %get-tuple-element.116.d0), channel_id=1, source_target_pairs={{0,8},{1,9},{2,10},{3,11},{4,12},{5,13},{6,14},{7,15},{8,0},{9,1},... | collective-permute-start | bytes 1179656 | tf_op jit(solution)/shard_map/ppermute | solution.py:538
  54.3 21.0 %collective-permute-start.14 = (bf16[4,192,256]{2,1,0:T(8,128)(2,1)}, bf16[4,192,256]{2,1,0:T(8,128)(2,1)S(1)}, u32[]{:S(2)}, u32[]{:S(2)}) collective-permute-start(bf16[4,192,256]{2,1,0:T(8,128)(2,1)} %get-tuple-element.116.d0), channel_id=1, source_target_pairs={{0,12},{1,13},{2,14},{3,15},{4,0},{5,1},{6,2},{7,3},{8,4},{9,5},{1... | collective-permute-start | bytes 1179656 | tf_op jit(solution)/shard_map/ppermute | solution.py:538
  56.8 3.3 %copy-start.15 = (bf16[3,512,128]{2,1,0:T(8,128)(2,1)}, bf16[3,512,128]{2,1,0:T(8,128)(2,1)S(1)}, u32[]{:S(2)}) copy-start(bf16[3,512,128]{2,1,0:T(8,128)(2,1)S(1)} %collective-permute-done.15.core_ref) | copy-start | bytes 1179652
  58.0 8.0 %collective-permute-start.16 = (bf16[3,256,128]{2,1,0:T(8,128)(2,1)S(1)}, bf16[3,256,128]{2,1,0:T(8,128)(2,1)S(1)}, u32[]{:S(2)}, u32[]{:S(2)}) collective-permute-start(bf16[3,256,128]{2,1,0:T(8,128)(2,1)S(1)} %add_convert_fusion), channel_id=1, source_target_pairs={{0,2},{1,3},{2,0},{3,1},{4,6},{5,7},{6,4},{7,5},{8,10},{9,11},{10,... | collective-permute-start | bytes 589832 | tf_op jit(solution)/shard_map/ppermute | solution.py:541
  66.0 0.7 copy-start.23
  66.7 8.6 %copy-start.3 = (bf16[4,192,256]{2,1,0:T(8,128)(2,1)S(1)}, bf16[4,192,256]{2,1,0:T(8,128)(2,1)}, u32[]{:S(2)}) copy-start(bf16[4,192,256]{2,1,0:T(8,128)(2,1)} %get-tuple-element.116.d0) | copy-start | bytes 1179652
  68.9 8.9 %collective-permute-start.18 = (bf16[4,3,64,128]{3,2,1,0:T(8,128)(2,1)}, bf16[4,3,64,128]{3,2,1,0:T(8,128)(2,1)S(1)}, u32[]{:S(2)}, u32[]{:S(2)}) collective-permute-start(bf16[4,3,64,128]{3,2,1,0:T(8,128)(2,1)} %finish_dkv.1.k0), channel_id=1, source_target_pairs={{0,4},{1,5},{2,6},{3,7},{4,8},{5,9},{6,10},{7,11},{8,12},{9,13},{1... | collective-permute-start | bytes 589832 | tf_op jit(solution)/shard_map/ppermute | solution.py:547
  68.9 10.6 %collective-permute-start.19 = (bf16[4,3,64,128]{3,2,1,0:T(8,128)(2,1)}, bf16[4,3,64,128]{3,2,1,0:T(8,128)(2,1)S(1)}, u32[]{:S(2)}, u32[]{:S(2)}) collective-permute-start(bf16[4,3,64,128]{3,2,1,0:T(8,128)(2,1)} %finish_dkv.1.k0), channel_id=1, source_target_pairs={{0,8},{1,9},{2,10},{3,11},{4,12},{5,13},{6,14},{7,15},{8,0},{9,1},... | collective-permute-start | bytes 589832 | tf_op jit(solution)/shard_map/ppermute | solution.py:547
  72.1 5.5 %copy-start.4 = (bf16[4,192,256]{2,1,0:T(8,128)(2,1)}, bf16[4,192,256]{2,1,0:T(8,128)(2,1)S(1)}, u32[]{:S(2)}) copy-start(bf16[4,192,256]{2,1,0:T(8,128)(2,1)S(1)} %collective-permute-done.12.d1) | copy-start | bytes 1179652
  72.1 10.6 %collective-permute-start.20 = (bf16[4,3,64,128]{3,2,1,0:T(8,128)(2,1)}, bf16[4,3,64,128]{3,2,1,0:T(8,128)(2,1)S(1)}, u32[]{:S(2)}, u32[]{:S(2)}) collective-permute-start(bf16[4,3,64,128]{3,2,1,0:T(8,128)(2,1)} %finish_dkv.1.k0), channel_id=1, source_target_pairs={{0,12},{1,13},{2,14},{3,15},{4,0},{5,1},{6,2},{7,3},{8,4},{9,5},{1... | collective-permute-start | bytes 589832 | tf_op jit(solution)/shard_map/ppermute | solution.py:547
  72.7 5.0 %copy-start.5 = (bf16[4,192,256]{2,1,0:T(8,128)(2,1)}, bf16[4,192,256]{2,1,0:T(8,128)(2,1)S(1)}, u32[]{:S(2)}) copy-start(bf16[4,192,256]{2,1,0:T(8,128)(2,1)S(1)} %collective-permute-done.13.d2) | copy-start | bytes 1179652
  75.3 2.4 %copy-start.6 = (bf16[4,192,256]{2,1,0:T(8,128)(2,1)}, bf16[4,192,256]{2,1,0:T(8,128)(2,1)S(1)}, u32[]{:S(2)}) copy-start(bf16[4,192,256]{2,1,0:T(8,128)(2,1)S(1)} %collective-permute-done.14.d3) | copy-start | bytes 1179652
  75.3 7.5 %copy-start.7 = (bf16[4,3,64,128]{3,2,1,0:T(8,128)(2,1)S(1)}, bf16[4,3,64,128]{3,2,1,0:T(8,128)(2,1)}, u32[]{:S(2)}) copy-start(bf16[4,3,64,128]{3,2,1,0:T(8,128)(2,1)} %finish_dkv.1.k0) | copy-start | bytes 589828
  77.7 6.7 %collective-permute-start.17 = (bf16[2,96,768]{2,1,0:T(8,128)(2,1)}, bf16[2,96,768]{2,1,0:T(8,128)(2,1)S(1)}, u32[]{:S(2)}, u32[]{:S(2)}) collective-permute-start(bf16[2,96,768]{2,1,0:T(8,128)(2,1)} %get-tuple-element.109), channel_id=1, source_target_pairs={{0,1},{1,0},{2,3},{3,2},{4,5},{5,4},{6,7},{7,6},{8,9},{9,8},{10,11... | collective-permute-start | bytes 884744 | tf_op jit(solution)/shard_map/ppermute | solution.py:507
  77.8 6.4 %copy-start.8 = (bf16[4,3,64,128]{3,2,1,0:T(8,128)(2,1)}, bf16[4,3,64,128]{3,2,1,0:T(8,128)(2,1)S(1)}, u32[]{:S(2)}) copy-start(bf16[4,3,64,128]{3,2,1,0:T(8,128)(2,1)S(1)} %collective-permute-done.18.k1) | copy-start | bytes 589828
  79.5 4.7 %copy-start.9 = (bf16[4,3,64,128]{3,2,1,0:T(8,128)(2,1)}, bf16[4,3,64,128]{3,2,1,0:T(8,128)(2,1)S(1)}, u32[]{:S(2)}) copy-start(bf16[4,3,64,128]{3,2,1,0:T(8,128)(2,1)S(1)} %collective-permute-done.19.k2) | copy-start | bytes 589828
  82.7 1.5 copy-start.10
  84.2 2.2 %collective-permute-start.21 = (bf16[2,96,1664]{2,1,0:T(8,128)(2,1)S(1)}, bf16[2,96,1664]{2,1,0:T(8,128)(2,1)S(1)}, u32[]{:S(2)}, u32[]{:S(2)}) collective-permute-start(bf16[2,96,1664]{2,1,0:T(8,128)(2,1)S(1)} %get-tuple-element.114), channel_id=1, source_target_pairs={{0,1},{1,0},{2,3},{3,2},{4,5},{5,4},{6,7},{7,6},{8,9},{9,8},{10,11... | collective-permute-start | bytes 1916936 | tf_op jit(solution)/shard_map/ppermute | solution.py:507
  86.6 14.3 %collective-permute-start.22 = (bf16[96,1664]{1,0:T(8,128)(2,1)S(1)}, bf16[96,1664]{1,0:T(8,128)(2,1)S(1)}, u32[]{:S(2)}, u32[]{:S(2)}) collective-permute-start(bf16[96,1664]{1,0:T(8,128)(2,1)S(1)} %fusion.1), channel_id=1, source_target_pairs={{0,2},{1,3},{2,0},{3,1},{4,6},{5,7},{6,4},{7,5},{8,10},{9,11},{10,... | collective-permute-start | bytes 958472 | tf_op jit(solution)/shard_map/ppermute | solution.py:556
  86.7 14.2 %collective-permute-start.23 = (bf16[96,768]{1,0:T(8,128)(2,1)S(1)}, bf16[96,768]{1,0:T(8,128)(2,1)S(1)}, u32[]{:S(2)}, u32[]{:S(2)}) collective-permute-start(bf16[96,768]{1,0:T(8,128)(2,1)S(1)} %fusion.3), channel_id=1, source_target_pairs={{0,2},{1,3},{2,0},{3,1},{4,6},{5,7},{6,4},{7,5},{8,10},{9,11},{10,... | collective-permute-start | bytes 442376 | tf_op jit(solution)/shard_map/ppermute | solution.py:555
  125.9 8.7 %copy-start.26 = (bf16[192,256]{1,0:T(8,128)(2,1)S(1)}, bf16[192,256]{1,0:T(8,128)(2,1)}, u32[]{:S(2)}) copy-start(bf16[192,256]{1,0:T(8,128)(2,1)} %get-tuple-element.122) | copy-start | bytes 294916
  125.9 9.2 %copy-start.25 = (bf16[192,256]{1,0:T(8,128)(2,1)S(1)}, bf16[192,256]{1,0:T(8,128)(2,1)}, u32[]{:S(2)}) copy-start(bf16[192,256]{1,0:T(8,128)(2,1)} %get-tuple-element.123) | copy-start | bytes 294916
  125.9 11.2 %copy-start.24 = (bf16[192,256]{1,0:T(8,128)(2,1)S(1)}, bf16[192,256]{1,0:T(8,128)(2,1)}, u32[]{:S(2)}) copy-start(bf16[192,256]{1,0:T(8,128)(2,1)} %get-tuple-element.124) | copy-start | bytes 294916
  125.9 16.5 %copy-start.14 = (bf16[192,256]{1,0:T(8,128)(2,1)S(1)}, bf16[192,256]{1,0:T(8,128)(2,1)}, u32[]{:S(2)}) copy-start(bf16[192,256]{1,0:T(8,128)(2,1)} %get-tuple-element.81) | copy-start | bytes 294916
  126.0 4.3 %collective-permute-start.27 = (bf16[24,1280]{1,0:T(8,128)(2,1)S(1)}, bf16[24,1280]{1,0:T(8,128)(2,1)S(1)}, u32[]{:S(2)}, u32[]{:S(2)}) collective-permute-start(bf16[24,1280]{1,0:T(8,128)(2,1)S(1)} %reduce_sum.12), channel_id=1, source_target_pairs={{0,128},{16,144},{32,160},{48,176},{64,192},{80,208},{96,224},{112... | collective-permute-start | bytes 184328 | tf_op jit(solution)/shard_map/ppermute | solution.py:574
  131.1 16.0 %all-to-all-start.1 = ((bf16[8,24,1152]{2,1,0:T(8,128)(2,1)}), bf16[8,24,1152]{2,1,0:T(8,128)(2,1)S(1)}, u32[]{:S(2)}, u32[]{:S(2)}) async-start(bf16[8,24,1152]{2,1,0:T(8,128)(2,1)} %broadcast_in_dim.8), calls=%async_computation.1 | async-start | bytes 884736 | tf_op jit(solution)/shard_map/all_to_all | solution.py:578
  134.6 4.7 %collective-permute-start.24 = (bf16[192,256]{1,0:T(8,128)(2,1)S(1)}, bf16[192,256]{1,0:T(8,128)(2,1)S(1)}, u32[]{:S(2)}, u32[]{:S(2)}) collective-permute-start(bf16[192,256]{1,0:T(8,128)(2,1)S(1)} %copy-done.26), channel_id=1, source_target_pairs={{0,12},{1,13},{2,14},{3,15},{4,0},{5,1},{6,2},{7,3},{8,4},{9,5},{1... | collective-permute-start | bytes 294920 | tf_op jit(solution)/shard_map/ppermute | solution.py:568
  135.1 6.1 %collective-permute-start.25 = (bf16[192,256]{1,0:T(8,128)(2,1)S(1)}, bf16[192,256]{1,0:T(8,128)(2,1)S(1)}, u32[]{:S(2)}, u32[]{:S(2)}) collective-permute-start(bf16[192,256]{1,0:T(8,128)(2,1)S(1)} %copy-done.25), channel_id=1, source_target_pairs={{0,8},{1,9},{2,10},{3,11},{4,12},{5,13},{6,14},{7,15},{8,0},{9,1},... | collective-permute-start | bytes 294920 | tf_op jit(solution)/shard_map/ppermute | solution.py:568
  137.1 5.4 %collective-permute-start.26 = (bf16[192,256]{1,0:T(8,128)(2,1)S(1)}, bf16[192,256]{1,0:T(8,128)(2,1)S(1)}, u32[]{:S(2)}, u32[]{:S(2)}) collective-permute-start(bf16[192,256]{1,0:T(8,128)(2,1)S(1)} %copy-done.24), channel_id=1, source_target_pairs={{0,4},{1,5},{2,6},{3,7},{4,8},{5,9},{6,10},{7,11},{8,12},{9,13},{1... | collective-permute-start | bytes 294920 | tf_op jit(solution)/shard_map/ppermute | solution.py:568
where the time goes:
time: 150 us; the launch traced here: 149 us
  Pallas kernels  38.7 us (26%)
  starting transfers between devices  37.3 us (25%)
  waiting for transfers between devices  36.9 us (25%)
  blocking collectives  24.6 us (16%)
  local copies, waits for them, and re-layouts  8.86 us (6%)
  other arithmetic  1.73 us (1%)
    all_to_all x1, blocking collectives, on_device(): shards = lax.all_to_all(chunks, 'dp', 0, 0, axis_index_groups=Z_GROUPS)  24.6 us
    pallas_call x1, Pallas kernels, attention(): pl.pallas_call(attention_kernel, in_specs=[smem()] + [vmem()] * 8, out_sp...  17.6 us
    ppermute x9, starting transfers between devices, spread_x(): lax.ppermute(parts[k], 'seq', X_SHIFT[k])  15.6 us
    ppermute x9, waiting for transfers between devices, spread_x(): lax.ppermute(parts[k], 'seq', X_SHIFT[k])  8.92 us
    pallas_call x1, Pallas kernels, grad_of_tokens(): pl.pallas_call(grad_tokens_kernel, grid_spec=grid_spec, out_shape=jax.Sha...  6.77 us
    ppermute x3, waiting for transfers between devices, on_device(): dkvs = [dkv] + [lax.ppermute(dkv, 'seq', X_SHIFT[k]) for k in range(1, 4)]  4.98 us
    pallas_call x1, Pallas kernels, keyval(): pl.pallas_call(keyval_kernel, in_specs=[smem(), smem(), hbm(), hbm(), hbm...  4.85 us
    unnamed x57, local copies, waits for them, and re-layouts  4.59 us
  transfers between devices with their start and end apart: 29, of which 16 were waited for; matrix products, arithmetic and copies ran while one was open for 3% of the time, Pallas kernels for 23%

commit v1 on v0

--- a/solution.py
+++ b/solution.py
@@ -200,7 +200,7 @@
 
 
 def attention_kernel(
-    x_ref, q0, q1, q2, q3, u0, u1, u2, u3, a0, a1, a2, a3, dq_ref, keep_ref, send_ref, kvn, kvt, qd, att, tables
+    x_ref, q0, q1, q2, q3, u0, u1, u2, u3, a0, a1, a2, a3, dq_ref, keep_ref, send_ref, kvn, kvt, qd, att, tables, pairs
 ):
     x = x_ref[0]
     for k, u in enumerate((u0, u1, u2, u3)):
@@ -218,13 +218,15 @@
         for k, table in enumerate(sub_tables(place[0:1], place[1:2], freq)):
             tables[p, pl.ds(16 * k, 16), :] = table
 
-    def step(h, carry):
-        at = pl.ds(pl.multiple_of(64 * h, 64), 64)
-        kv = kvn[h]
-        kv_t = kvt[h]
+    def step(i, carry):
         total = None
         outs = []
-        for p in range(4):
+        for j in range(6):
+            h = (6 * i + j) // 4
+            p = (6 * i + j) % 4
+            at = pl.ds(pl.multiple_of(64 * h, 64), 64)
+            kv = kvn[h]
+            kv_t = kvt[h]
             q = qd[p, at, :]
             do = qd[p, pl.ds(pl.multiple_of(GROUP + 64 * h, 64), 64), :]
             zero = jnp.zeros_like(q)
@@ -243,17 +245,21 @@
             dscore = (prob * (dprob - delta)).astype(BF16)
             dq = mm(kv_t[0:64], dscore) * 0.125
             table = [tables[p, pl.ds(16 * k, 16), :] for k in range(4)]
-            outs.append((mixed, sub_turn(dq, table, -1.0).astype(BF16)))
+            outs.append((p, at, mixed, sub_turn(dq, table, -1.0).astype(BF16)))
             part = mm(dscore, q_pad, ((1,), (1,))) + mm(prob.astype(BF16), do_pad, ((1,), (1,)))
-            total = part if total is None else total + part
-        for p, (mixed, dq) in enumerate(outs):
+            total = part if j % 2 == 0 else total + part
+            if j % 2 == 1:
+                pairs[3 * i + j // 2] = total
+        for p, at, mixed, dq in outs:
             att[p, at, :] = mixed
             dq_ref[(x + 4 - p) % 4, at, :] = dq
+        return carry
+
+    lax.fori_loop(0, 2, step, 0)
+    for h in range(3):
+        total = pairs[2 * h] + pairs[2 * h + 1]
         keep_ref[h] = total[0:512]
         send_ref[h] = total[512:1024].astype(BF16)
-        return carry
-
-    lax.fori_loop(0, 3, step, 0)
     for d, a in enumerate((a0, a1, a2, a3)):
         a[...] = att[d]
 
@@ -276,6 +282,7 @@
             pltpu.VMEM((4, MSG, TOK), BF16),
             pltpu.VMEM((4, GROUP, TOK), BF16),
             pltpu.VMEM((4, 64, TOK), F32),
+            pltpu.VMEM((6, 1024, 128), F32),
         ],
         compiler_params=params(56),
         cost_estimate=cost(20),
@@ -529,9 +536,9 @@
     unit_y = lax.ppermute(unit, "seq", Y_SWAP)
     unit_cy = lax.ppermute(unit_y, "seq", CORE_SWAP)
 
-    held = after(own, qs[1])
+    held = own
     slices = [lax.dynamic_slice(held, (0, ROWS * ((x + k) % 4)), (TOK, ROWS)) for k in range(4)]
-    toks = spread_x(slices)
+    toks = spread_x(after(slices, qs[1]))
 
     a0, a1, a2, a3, dq, keep, send = attention(xs, qs, [unit, unit_y, unit_c, unit_cy])
     dq, keep, send, toks = lax.optimization_barrier((dq, keep, send, toks))

time: 150 us -> 149 us (level)
  transfers between devices with their start and end apart: 29 -> 29, of which waited for: 16 -> 16; matrix products, arithmetic and copies ran while one was open for 3% -> 4% of each run, Pallas kernels for 23% -> 22%
where the time goes in v1:
time: 149 us
  Pallas kernels  38.3 us (26%)
  starting transfers between devices  37.4 us (25%)
  waiting for transfers between devices  35.8 us (24%)
  blocking collectives  24.6 us (17%)
  local copies, waits for them, and re-layouts  8.86 us (6%)
  other arithmetic  2.69 us (2%)
    all_to_all x1, blocking collectives, on_device(): shards = lax.all_to_all(chunks, 'dp', 0, 0, axis_index_groups=Z_GROUPS)  24.6 us
    pallas_call x1, Pallas kernels, attention(): pl.pallas_call(attention_kernel, in_specs=[smem()] + [vmem()] * 8, out_sp...  17.1 us
    ppermute x9, starting transfers between devices, spread_x(): lax.ppermute(parts[k], 'seq', X_SHIFT[k])  15.7 us
    ppermute x9, waiting for transfers between devices, spread_x(): lax.ppermute(parts[k], 'seq', X_SHIFT[k])  8.82 us
    pallas_call x1, Pallas kernels, grad_of_tokens(): pl.pallas_call(grad_tokens_kernel, grid_spec=grid_spec, out_shape=jax.Sha...  6.77 us
    ppermute x3, waiting for transfers between devices, on_device(): dkvs = [dkv] + [lax.ppermute(dkv, 'seq', X_SHIFT[k]) for k in range(1, 4)]  4.98 us
    pallas_call x1, Pallas kernels, keyval(): pl.pallas_call(keyval_kernel, in_specs=[smem(), smem(), hbm(), hbm(), hbm...  4.85 us
    unnamed x57, local copies, waits for them, and re-layouts  4.59 us
  transfers between devices with their start and end apart: 29, of which 16 were waited for; matrix products, arithmetic and copies ran while one was open for 4% of the time, Pallas kernels for 22%

profile of v1, /device:TPU:2, one launch (start us, length us, event | category | flops | bytes accessed | tf_op | source)
XLA Modules:
  0.0 148.8 jit_solution(8931087042346090794)
XLA Ops:
  0.7 4.8 %keyval.1 = (bf16[3,64,128]{2,1,0:T(8,128)(2,1)}, bf16[3,64,128]{2,1,0:T(8,128)(2,1)}, bf16[3,64,128]{2,1,0:T(8,128)(2,1)}, bf16[3,64,128]{2,1,0:T(8,128)(2,1)}) custom-call(s32[1]{0:T(128)} %bitcast.x_ref, s32[256]{0:T(256)} %bitcast.63, bf16[256,1536]{1,0:T(8,128)(2,1)} %bitcast.60, f32[4,1536]{1,0:T(4,128)} %wm_ref.1, bf16[1536,1536]{1,0:T(8,128)(2,1)} %wkv_ref.3), custom_call_target="tpu_custom_call" | custom-call | flops 6600000000 | bytes 600000 | tf_op jit(solution)/shard_map/keyval/pallas_call | solution.py:119
  5.5 1.6 %collective-permute-start = (bf16[3,64,128]{2,1,0:T(8,128)(2,1)}, bf16[3,64,128]{2,1,0:T(8,128)(2,1)S(1)}, u32[]{:S(2)}, u32[]{:S(2)}) collective-permute-start(bf16[3,64,128]{2,1,0:T(8,128)(2,1)} %get-tuple-element.69), channel_id=1, source_target_pairs={{0,4},{1,5},{2,6},{3,7},{4,8},{5,9},{6,10},{7,11},{8,12},{9,13},{1... | collective-permute-start | bytes 147464 | tf_op jit(solution)/shard_map/ppermute | solution.py:506
  7.1 2.8 %collective-permute-start.1 = (bf16[3,64,128]{2,1,0:T(8,128)(2,1)}, bf16[3,64,128]{2,1,0:T(8,128)(2,1)S(1)}, u32[]{:S(2)}, u32[]{:S(2)}) collective-permute-start(bf16[3,64,128]{2,1,0:T(8,128)(2,1)} %get-tuple-element.70), channel_id=1, source_target_pairs={{0,8},{1,9},{2,10},{3,11},{4,12},{5,13},{6,14},{7,15},{8,0},{9,1},... | collective-permute-start | bytes 147464 | tf_op jit(solution)/shard_map/ppermute | solution.py:506
  10.0 0.4 collective-permute-start.2
  10.4 1.0 queries.1
  11.5 1.5 collective-permute-done.1
  12.9 1.3 collective-permute-done.2
  14.3 2.1 %collective-permute-start.6 = (bf16[4,3,64,128]{3,2,1,0:T(8,128)(2,1)S(1)}, bf16[4,3,64,128]{3,2,1,0:T(8,128)(2,1)S(1)}, u32[]{:S(2)}, u32[]{:S(2)}) collective-permute-start(bf16[4,3,64,128]{3,2,1,0:T(8,128)(2,1)S(1)} %pad_maximum_fusion.2.u0), channel_id=1, source_target_pairs={{0,2},{1,3},{2,0},{3,1},{4,6},{5,7},{6,4},{7,5},{8,10},{9,11},{10,... | collective-permute-start | bytes 589832 | tf_op jit(solution)/shard_map/ppermute | solution.py:536
  16.4 1.1 collective-permute-start.3
  17.4 2.6 %collective-permute-start.4 = (bf16[400,256]{1,0:T(8,128)(2,1)S(1)}, bf16[400,256]{1,0:T(8,128)(2,1)S(1)}, u32[]{:S(2)}, u32[]{:S(2)}) collective-permute-start(bf16[400,256]{1,0:T(8,128)(2,1)S(1)} %get-tuple-element.78), channel_id=1, source_target_pairs={{0,8},{1,9},{2,10},{3,11},{4,12},{5,13},{6,14},{7,15},{8,0},{9,1},... | collective-permute-start | bytes 614408 | tf_op jit(solution)/shard_map/ppermute | solution.py:506
  20.1 2.0 %collective-permute-start.5 = (bf16[400,256]{1,0:T(8,128)(2,1)S(1)}, bf16[400,256]{1,0:T(8,128)(2,1)S(1)}, u32[]{:S(2)}, u32[]{:S(2)}) collective-permute-start(bf16[400,256]{1,0:T(8,128)(2,1)S(1)} %get-tuple-element.79), channel_id=1, source_target_pairs={{0,12},{1,13},{2,14},{3,15},{4,0},{5,1},{6,2},{7,3},{8,4},{9,5},{1... | collective-permute-start | bytes 614408 | tf_op jit(solution)/shard_map/ppermute | solution.py:506
  22.1 0.5 collective-permute-start.8
  22.7 1.3 collective-permute-done.3.q1
  24.0 2.7 %collective-permute-start.10 = (bf16[256,384]{1,0:T(8,128)(2,1)S(1)}, bf16[256,384]{1,0:T(8,128)(2,1)S(1)}, u32[]{:S(2)}, u32[]{:S(2)}) collective-permute-start(bf16[256,384]{1,0:T(8,128)(2,1)S(1)} %get-tuple-element.93), channel_id=1, source_target_pairs={{0,8},{1,9},{2,10},{3,11},{4,12},{5,13},{6,14},{7,15},{8,0},{9,1},... | collective-permute-start | bytes 589832 | tf_op jit(solution)/shard_map/ppermute | solution.py:506
  26.7 0.6 collective-permute-start.11
  27.3 1.8 %collective-permute-start.9 = (bf16[256,384]{1,0:T(8,128)(2,1)S(1)}, bf16[256,384]{1,0:T(8,128)(2,1)S(1)}, u32[]{:S(2)}, u32[]{:S(2)}) collective-permute-start(bf16[256,384]{1,0:T(8,128)(2,1)S(1)} %get-tuple-element.92), channel_id=1, source_target_pairs={{0,4},{1,5},{2,6},{3,7},{4,8},{5,9},{6,10},{7,11},{8,12},{9,13},{1... | collective-permute-start | bytes 589832 | tf_op jit(solution)/shard_map/ppermute | solution.py:506
  29.2 4.7 %collective-permute-done.5.q3 = bf16[400,256]{1,0:T(8,128)(2,1)S(1)} collective-permute-done((bf16[400,256]{1,0:T(8,128)(2,1)S(1)}, bf16[400,256]{1,0:T(8,128)(2,1)S(1)}, u32[]{:S(2)}, u32[]{:S(2)}) %collective-permute-start.5) | collective-permute-done | bytes 204832 | tf_op jit(solution)/shard_map/ppermute | solution.py:506
  33.9 0.6 copy-done.19
  34.5 0.7 copy-done.22
  35.2 17.1 %attention.1 = (bf16[192,256]{1,0:T(8,128)(2,1)}, bf16[192,256]{1,0:T(8,128)(2,1)}, bf16[192,256]{1,0:T(8,128)(2,1)}, bf16[192,256]{1,0:T(8,128)(2,1)}, bf16[4,1...) custom-call(s32[1]{0:T(128)} %bitcast.x_ref, bf16[400,256]{1,0:T(8,128)(2,1)} %copy-done.12, ...), custom_call_target="tpu_custom_call" | custom-call | flops 22000001024 | bytes 2000000 | tf_op jit(solution)/shard_map/attention/pallas_call | solution.py:269
  52.3 0.1 collective-permute-start.15
  52.5 1.3 collective-permute-start.13
  53.8 2.5 %collective-permute-start.14 = (bf16[4,192,256]{2,1,0:T(8,128)(2,1)}, bf16[4,192,256]{2,1,0:T(8,128)(2,1)S(1)}, u32[]{:S(2)}, u32[]{:S(2)}) collective-permute-start(bf16[4,192,256]{2,1,0:T(8,128)(2,1)} %get-tuple-element.122.d0), channel_id=1, source_target_pairs={{0,12},{1,13},{2,14},{3,15},{4,0},{5,1},{6,2},{7,3},{8,4},{9,5},{1... | collective-permute-start | bytes 1179656 | tf_op jit(solution)/shard_map/ppermute | solution.py:545
  56.4 1.2 add_convert_fusion
  57.5 0.1 collective-permute-start.16
  57.6 0.7 constant_dynamic-slice_fusion.1.wm_ref
  58.3 1.3 constant_dynamic-slice_fusion.wkv_ref
  59.7 2.5 %key_tables.1 = (f32[256,128]{1,0:T(8,128)}, f32[256,128]{1,0:T(8,128)}) custom-call(bf16[400,256]{1,0:T(8,128)(2,1)} %copy-done.12, bf16[400,256]{1,0:T(8,128)(2,1)} %copy-done.17, bf16[400,256]{1,0:T(8,128)(2,1)} %copy-done.18, bf16[400,256]{1,0:T(8,128)(2,1)} %copy-done.19), custom_call_target="tpu_custom_call" | custom-call | flops 2200000000 | bytes 200000 | tf_op jit(solution)/shard_map/key_tables/pallas_call | solution.py:310
  62.2 3.4 %collective-permute-done.16.y_ref = bf16[3,256,128]{2,1,0:T(8,128)(2,1)S(1)} collective-permute-done((bf16[3,256,128]{2,1,0:T(8,128)(2,1)S(1)}, bf16[3,256,128]{2,1,0:T(8,128)(2,1)S(1)}, u32[]{:S(2)}, u32[]{:S(2)}) %collective-permute-start.16) | collective-permute-done | bytes 196640 | tf_op jit(solution)/shard_map/ppermute | solution.py:548
  65.5 0.7 copy-done.23
  66.2 2.3 %finish_dkv.1.k0 = bf16[4,3,64,128]{3,2,1,0:T(8,128)(2,1)} custom-call(s32[1]{0:T(128)} %bitcast.x_ref, f32[256,128]{1,0:T(8,128)} %get-tuple-element.106.cos_ref, f32[256,128]{1,0:T(8,128)} %get-tuple-element.107.sin_ref, f32[3,512,128]{2,1,0:T(8,128)} %get-tuple-element.100.keep_ref, bf16[3,512,128]{2,1,0:T(8,128)(2,1)} %copy-done.15, ...), custom_call_target="tpu_custom_call" | custom-call | flops 2200000000 | bytes 200000 | tf_op jit(solution)/shard_map/finish_dkv/pallas_call | solution.py:333
  68.5 3.2 %collective-permute-start.19 = (bf16[4,3,64,128]{3,2,1,0:T(8,128)(2,1)}, bf16[4,3,64,128]{3,2,1,0:T(8,128)(2,1)S(1)}, u32[]{:S(2)}, u32[]{:S(2)}) collective-permute-start(bf16[4,3,64,128]{3,2,1,0:T(8,128)(2,1)} %finish_dkv.1.k0), channel_id=1, source_target_pairs={{0,8},{1,9},{2,10},{3,11},{4,12},{5,13},{6,14},{7,15},{8,0},{9,1},... | collective-permute-start | bytes 589832 | tf_op jit(solution)/shard_map/ppermute | solution.py:554
  71.6 0.6 collective-permute-start.20
  72.2 2.5 %collective-permute-done.14.d3 = bf16[4,192,256]{2,1,0:T(8,128)(2,1)S(1)} collective-permute-done((bf16[4,192,256]{2,1,0:T(8,128)(2,1)}, bf16[4,192,256]{2,1,0:T(8,128)(2,1)S(1)}, u32[]{:S(2)}, u32[]{:S(2)}) %collective-permute-start.14) | collective-permute-done | bytes 393248 | tf_op jit(solution)/shard_map/ppermute | solution.py:545
  74.8 2.4 %term_q.1 = (f32[2,96,768]{2,1,0:T(8,128)S(1)}, bf16[2,96,768]{2,1,0:T(8,128)(2,1)}, f32[3,1024,128]{2,1,0:T(8,128)S(1)}, bf16[256,384]{1,0:T(8,128)(2,1)S(1)}) custom-call(s32[1]{0:T(128)} %bitcast.x_ref, s32[1]{0:T(128)} %bitcast.9.c_ref, bf16[256,384]{1,0:T(8,128)(2,1)S(1)} %get-tuple-element.95.t0, bf16[256,384]{1,0:T(8,128)(2,1)S(1)} %collective-permute-done.9.t1, ...), custom_call_target="tpu_custom_call" | custom-call | flops 4400000000 | bytes 400000 | tf_op jit(solution)/shard_map/term_q/pallas_call | solution.py:368
  77.3 1.7 %collective-permute-done.19.k2 = bf16[4,3,64,128]{3,2,1,0:T(8,128)(2,1)S(1)} collective-permute-done((bf16[4,3,64,128]{3,2,1,0:T(8,128)(2,1)}, bf16[4,3,64,128]{3,2,1,0:T(8,128)(2,1)S(1)}, u32[]{:S(2)}, u32[]{:S(2)}) %collective-permute-start.19) | collective-permute-done | bytes 196640 | tf_op jit(solution)/shard_map/ppermute | solution.py:554
  79.0 3.2 %collective-permute-done.20.k3 = bf16[4,3,64,128]{3,2,1,0:T(8,128)(2,1)S(1)} collective-permute-done((bf16[4,3,64,128]{3,2,1,0:T(8,128)(2,1)}, bf16[4,3,64,128]{3,2,1,0:T(8,128)(2,1)S(1)}, u32[]{:S(2)}, u32[]{:S(2)}) %collective-permute-start.20) | collective-permute-done | bytes 196640 | tf_op jit(solution)/shard_map/ppermute | solution.py:554
  82.2 1.5 term_kv.1
  83.7 0.1 collective-permute-start.21
  83.9 1.0 convert_add_fusion.1
  84.9 1.0 collective-permute-done.21
  85.9 0.1 convert_add_fusion
  86.0 0.1 collective-permute-start.22
  86.2 3.5 %collective-permute-start.23 = (bf16[96,768]{1,0:T(8,128)(2,1)S(1)}, bf16[96,768]{1,0:T(8,128)(2,1)S(1)}, u32[]{:S(2)}, u32[]{:S(2)}) collective-permute-start(bf16[96,768]{1,0:T(8,128)(2,1)S(1)} %fusion.3), channel_id=1, source_target_pairs={{0,2},{1,3},{2,0},{3,1},{4,6},{5,7},{6,4},{7,5},{8,10},{9,11},{10,... | collective-permute-start | bytes 442376 | tf_op jit(solution)/shard_map/ppermute | solution.py:562
  89.7 6.8 %grad_tokens.1 = bf16[1,256,1536]{2,1,0:T(8,128)(2,1)} custom-call(s32[1]{0:T(128)} %bitcast.x_ref, bf16[4,192,256]{2,1,0:T(8,128)(2,1)} %get-tuple-element.122.d0, bf16[4,192,256]{2,1,0:T(8,128)(2,1)} %copy-done.4, bf16[4,192,256]{2,1,0:T(8,128)(2,1)} %copy-done.5, bf16[4,192,256]{2,1,0:T(8,128)(2,1)} %copy-done.6, bf16[4,3,64,128]{3,2,1,0:T(8,128)(2,1)} %finish_dkv.1.k0, ...), custom_call_target="tpu_custom_call" | custom-call | flops 6600000000 | bytes 600000 | tf_op jit(solution)/shard_map/grad_tokens/pallas_call | solution.py:495
  96.4 3.9 %collective-permute-done.23 = bf16[96,768]{1,0:T(8,128)(2,1)S(1)} collective-permute-done((bf16[96,768]{1,0:T(8,128)(2,1)S(1)}, bf16[96,768]{1,0:T(8,128)(2,1)S(1)}, u32[]{:S(2)}, u32[]{:S(2)}) %collective-permute-start.23) | collective-permute-done | bytes 147488 | tf_op jit(solution)/shard_map/ppermute | solution.py:562
  100.8 24.6 %all_to_all.10 = bf16[8,24,1280]{2,1,0:T(8,128)(2,1)S(1)} all-to-all(bf16[8,24,1280]{2,1,0:T(8,128)(2,1)S(1)} %pad_maximum_fusion), channel_id=1, replica_groups={{0,16,32,48,64,80,96,112},{128,144,160,176,192,208,224,240},{1,17,33,49..., dimensions={0} | all-to-all | bytes 983040 | tf_op jit(solution)/shard_map/all_to_all | solution.py:573
  125.5 0.1 collective-permute-start.27
  125.6 4.2 %collective-permute-done.27 = bf16[24,1280]{1,0:T(8,128)(2,1)S(1)} collective-permute-done((bf16[24,1280]{1,0:T(8,128)(2,1)S(1)}, bf16[24,1280]{1,0:T(8,128)(2,1)S(1)}, u32[]{:S(2)}, u32[]{:S(2)}) %collective-permute-start.27) | collective-permute-done | bytes 61472 | tf_op jit(solution)/shard_map/ppermute | solution.py:581
  129.9 0.8 broadcast_in_dim.8
  130.6 3.5 %all-to-all-start.1 = ((bf16[8,24,1152]{2,1,0:T(8,128)(2,1)}), bf16[8,24,1152]{2,1,0:T(8,128)(2,1)S(1)}, u32[]{:S(2)}, u32[]{:S(2)}) async-start(bf16[8,24,1152]{2,1,0:T(8,128)(2,1)} %broadcast_in_dim.8), calls=%async_computation.1 | async-start | bytes 884736 | tf_op jit(solution)/shard_map/all_to_all | solution.py:585
  134.1 0.5 collective-permute-start.24
  134.6 2.0 %collective-permute-start.25 = (bf16[192,256]{1,0:T(8,128)(2,1)S(1)}, bf16[192,256]{1,0:T(8,128)(2,1)S(1)}, u32[]{:S(2)}, u32[]{:S(2)}) collective-permute-start(bf16[192,256]{1,0:T(8,128)(2,1)S(1)} %copy-done.25), channel_id=1, source_target_pairs={{0,8},{1,9},{2,10},{3,11},{4,12},{5,13},{6,14},{7,15},{8,0},{9,1},... | collective-permute-start | bytes 294920 | tf_op jit(solution)/shard_map/ppermute | solution.py:575
  136.6 1.5 %collective-permute-start.26 = (bf16[192,256]{1,0:T(8,128)(2,1)S(1)}, bf16[192,256]{1,0:T(8,128)(2,1)S(1)}, u32[]{:S(2)}, u32[]{:S(2)}) collective-permute-start(bf16[192,256]{1,0:T(8,128)(2,1)S(1)} %copy-done.24), channel_id=1, source_target_pairs={{0,4},{1,5},{2,6},{3,7},{4,8},{5,9},{6,10},{7,11},{8,12},{9,13},{1... | collective-permute-start | bytes 294920 | tf_op jit(solution)/shard_map/ppermute | solution.py:575
  138.1 0.7 collective-permute-done.24
  138.8 1.9 %collective-permute-done.25 = bf16[192,256]{1,0:T(8,128)(2,1)S(1)} collective-permute-done((bf16[192,256]{1,0:T(8,128)(2,1)S(1)}, bf16[192,256]{1,0:T(8,128)(2,1)S(1)}, u32[]{:S(2)}, u32[]{:S(2)}) %collective-permute-start.25) | collective-permute-done | bytes 98336 | tf_op jit(solution)/shard_map/ppermute | solution.py:575
  140.7 1.2 collective-permute-done.26
  142.1 0.9 copy.18
  143.0 0.6 slice.39
  143.6 3.1 %all-to-all-done.1 = bf16[8,24,1152]{2,1,0:T(8,128)(2,1)S(1)} async-done(((bf16[8,24,1152]{2,1,0:T(8,128)(2,1)}), bf16[8,24,1152]{2,1,0:T(8,128)(2,1)S(1)}, u32[]{:S(2)}, u32[]{:S(2)}) %all-to-all-start.1) | async-done | bytes 442400 | tf_op jit(solution)/shard_map/all_to_all | solution.py:585
  146.7 0.3 copy.17
  147.0 0.9 copy.20
  147.9 0.2 copy.16
  148.1 0.7 copy.19
  (91 shorter events, 1.2 us)
Async XLA Ops:
  0.6 9.7 %copy-start = (bf16[1,256,1536]{2,1,0:T(8,128)(2,1)S(1)}, bf16[1,256,1536]{2,1,0:T(8,128)(2,1)}, u32[]{:S(2)}) copy-start(bf16[1,256,1536]{2,1,0:T(8,128)(2,1)} %param.6) | copy-start | bytes 2359300
  0.7 9.7 %copy-start.1 = (bf16[1536,768]{1,0:T(8,128)(2,1)S(1)}, bf16[1536,768]{1,0:T(8,128)(2,1)}, u32[]{:S(2)}) copy-start(bf16[1536,768]{1,0:T(8,128)(2,1)} %wq_ref.3) | copy-start | bytes 7077892
  0.7 9.7 %copy-start.2 = (bf16[1,256,768]{2,1,0:T(8,128)(2,1)S(1)}, bf16[1,256,768]{2,1,0:T(8,128)(2,1)}, u32[]{:S(2)}) copy-start(bf16[1,256,768]{2,1,0:T(8,128)(2,1)} %param.8) | copy-start | bytes 1179652
  0.7 9.7 %copy-start.11 = (s32[1,256]{1,0:T(1,128)S(1)}, s32[1,256]{1,0:T(1,128)}, u32[]{:S(2)}) copy-start(s32[1,256]{1,0:T(1,128)} %idx_ref.1) | copy-start | bytes 3076
  5.5 5.9 %collective-permute-start = (bf16[3,64,128]{2,1,0:T(8,128)(2,1)}, bf16[3,64,128]{2,1,0:T(8,128)(2,1)S(1)}, u32[]{:S(2)}, u32[]{:S(2)}) collective-permute-start(bf16[3,64,128]{2,1,0:T(8,128)(2,1)} %get-tuple-element.69), channel_id=1, source_target_pairs={{0,4},{1,5},{2,6},{3,7},{4,8},{5,9},{6,10},{7,11},{8,12},{9,13},{1... | collective-permute-start | bytes 147464 | tf_op jit(solution)/shard_map/ppermute | solution.py:506
  7.1 5.8 %collective-permute-start.1 = (bf16[3,64,128]{2,1,0:T(8,128)(2,1)}, bf16[3,64,128]{2,1,0:T(8,128)(2,1)S(1)}, u32[]{:S(2)}, u32[]{:S(2)}) collective-permute-start(bf16[3,64,128]{2,1,0:T(8,128)(2,1)} %get-tuple-element.70), channel_id=1, source_target_pairs={{0,8},{1,9},{2,10},{3,11},{4,12},{5,13},{6,14},{7,15},{8,0},{9,1},... | collective-permute-start | bytes 147464 | tf_op jit(solution)/shard_map/ppermute | solution.py:506
  10.0 4.3 %collective-permute-start.2 = (bf16[3,64,128]{2,1,0:T(8,128)(2,1)}, bf16[3,64,128]{2,1,0:T(8,128)(2,1)S(1)}, u32[]{:S(2)}, u32[]{:S(2)}) collective-permute-start(bf16[3,64,128]{2,1,0:T(8,128)(2,1)} %get-tuple-element.71), channel_id=1, source_target_pairs={{0,12},{1,13},{2,14},{3,15},{4,0},{5,1},{6,2},{7,3},{8,4},{9,5},{1... | collective-permute-start | bytes 147464 | tf_op jit(solution)/shard_map/ppermute | solution.py:506
  10.4 3.9 %copy-start.16 = (bf16[3,64,128]{2,1,0:T(8,128)(2,1)S(1)}, bf16[3,64,128]{2,1,0:T(8,128)(2,1)}, u32[]{:S(2)}) copy-start(bf16[3,64,128]{2,1,0:T(8,128)(2,1)} %get-tuple-element.80) | copy-start | bytes 147460
  11.4 10.7 %copy-start.12 = (bf16[400,256]{1,0:T(8,128)(2,1)}, bf16[400,256]{1,0:T(8,128)(2,1)S(1)}, u32[]{:S(2)}) copy-start(bf16[400,256]{1,0:T(8,128)(2,1)S(1)} %get-tuple-element.102.q0) | copy-start | bytes 614404
  14.3 19.6 %copy-start.13 = (bf16[4,3,64,128]{3,2,1,0:T(8,128)(2,1)}, bf16[4,3,64,128]{3,2,1,0:T(8,128)(2,1)S(1)}, u32[]{:S(2)}) copy-start(bf16[4,3,64,128]{3,2,1,0:T(8,128)(2,1)S(1)} %pad_maximum_fusion.2.u0) | copy-start | bytes 589828
  14.3 7.8 %collective-permute-start.6 = (bf16[4,3,64,128]{3,2,1,0:T(8,128)(2,1)S(1)}, bf16[4,3,64,128]{3,2,1,0:T(8,128)(2,1)S(1)}, u32[]{:S(2)}, u32[]{:S(2)}) collective-permute-start(bf16[4,3,64,128]{3,2,1,0:T(8,128)(2,1)S(1)} %pad_maximum_fusion.2.u0), channel_id=1, source_target_pairs={{0,2},{1,3},{2,0},{3,1},{4,6},{5,7},{6,4},{7,5},{8,10},{9,11},{10,... | collective-permute-start | bytes 589832 | tf_op jit(solution)/shard_map/ppermute | solution.py:536
  16.4 7.6 %collective-permute-start.3 = (bf16[400,256]{1,0:T(8,128)(2,1)S(1)}, bf16[400,256]{1,0:T(8,128)(2,1)S(1)}, u32[]{:S(2)}, u32[]{:S(2)}) collective-permute-start(bf16[400,256]{1,0:T(8,128)(2,1)S(1)} %get-tuple-element.77), channel_id=1, source_target_pairs={{0,4},{1,5},{2,6},{3,7},{4,8},{5,9},{6,10},{7,11},{8,12},{9,13},{1... | collective-permute-start | bytes 614408 | tf_op jit(solution)/shard_map/ppermute | solution.py:506
  17.4 9.9 %collective-permute-start.4 = (bf16[400,256]{1,0:T(8,128)(2,1)S(1)}, bf16[400,256]{1,0:T(8,128)(2,1)S(1)}, u32[]{:S(2)}, u32[]{:S(2)}) collective-permute-start(bf16[400,256]{1,0:T(8,128)(2,1)S(1)} %get-tuple-element.78), channel_id=1, source_target_pairs={{0,8},{1,9},{2,10},{3,11},{4,12},{5,13},{6,14},{7,15},{8,0},{9,1},... | collective-permute-start | bytes 614408 | tf_op jit(solution)/shard_map/ppermute | solution.py:506
  20.1 13.8 %collective-permute-start.5 = (bf16[400,256]{1,0:T(8,128)(2,1)S(1)}, bf16[400,256]{1,0:T(8,128)(2,1)S(1)}, u32[]{:S(2)}, u32[]{:S(2)}) collective-permute-start(bf16[400,256]{1,0:T(8,128)(2,1)S(1)} %get-tuple-element.79), channel_id=1, source_target_pairs={{0,12},{1,13},{2,14},{3,15},{4,0},{5,1},{6,2},{7,3},{8,4},{9,5},{1... | collective-permute-start | bytes 614408 | tf_op jit(solution)/shard_map/ppermute | solution.py:506
  22.1 4.6 %collective-permute-start.7 = (bf16[4,3,64,128]{3,2,1,0:T(8,128)(2,1)S(1)}, bf16[4,3,64,128]{3,2,1,0:T(8,128)(2,1)S(1)}, u32[]{:S(2)}, u32[]{:S(2)}) collective-permute-start(bf16[4,3,64,128]{3,2,1,0:T(8,128)(2,1)S(1)} %pad_maximum_fusion.2.u0), channel_id=1, source_target_pairs={{0,1},{1,0},{2,3},{3,2},{4,5},{5,4},{6,7},{7,6},{8,9},{9,8},{10,11... | collective-permute-start | bytes 589832 | tf_op jit(solution)/shard_map/ppermute | solution.py:535
  22.1 11.7 %copy-start.20 = (bf16[4,3,64,128]{3,2,1,0:T(8,128)(2,1)}, bf16[4,3,64,128]{3,2,1,0:T(8,128)(2,1)S(1)}, u32[]{:S(2)}) copy-start(bf16[4,3,64,128]{3,2,1,0:T(8,128)(2,1)S(1)} %collective-permute-done.6.u1) | copy-start | bytes 589828
  22.1 11.7 %collective-permute-start.8 = (bf16[4,3,64,128]{3,2,1,0:T(8,128)(2,1)S(1)}, bf16[4,3,64,128]{3,2,1,0:T(8,128)(2,1)S(1)}, u32[]{:S(2)}, u32[]{:S(2)}) collective-permute-start(bf16[4,3,64,128]{3,2,1,0:T(8,128)(2,1)S(1)} %collective-permute-done.6.u1), channel_id=1, source_target_pairs={{0,1},{1,0},{2,3},{3,2},{4,5},{5,4},{6,7},{7,6},{8,9},{9,8},{10,11... | collective-permute-start | bytes 589832 | tf_op jit(solution)/shard_map/ppermute | solution.py:537
  24.0 9.9 %copy-start.17 = (bf16[400,256]{1,0:T(8,128)(2,1)}, bf16[400,256]{1,0:T(8,128)(2,1)S(1)}, u32[]{:S(2)}) copy-start(bf16[400,256]{1,0:T(8,128)(2,1)S(1)} %collective-permute-done.3.q1) | copy-start | bytes 614404
  24.0 28.3 %collective-permute-start.10 = (bf16[256,384]{1,0:T(8,128)(2,1)S(1)}, bf16[256,384]{1,0:T(8,128)(2,1)S(1)}, u32[]{:S(2)}, u32[]{:S(2)}) collective-permute-start(bf16[256,384]{1,0:T(8,128)(2,1)S(1)} %get-tuple-element.93), channel_id=1, source_target_pairs={{0,8},{1,9},{2,10},{3,11},{4,12},{5,13},{6,14},{7,15},{8,0},{9,1},... | collective-permute-start | bytes 589832 | tf_op jit(solution)/shard_map/ppermute | solution.py:506
  26.7 7.2 %copy-start.21 = (bf16[4,3,64,128]{3,2,1,0:T(8,128)(2,1)}, bf16[4,3,64,128]{3,2,1,0:T(8,128)(2,1)S(1)}, u32[]{:S(2)}) copy-start(bf16[4,3,64,128]{3,2,1,0:T(8,128)(2,1)S(1)} %collective-permute-done.7.u2) | copy-start | bytes 589828
  26.7 25.6 %collective-permute-start.11 = (bf16[256,384]{1,0:T(8,128)(2,1)S(1)}, bf16[256,384]{1,0:T(8,128)(2,1)S(1)}, u32[]{:S(2)}, u32[]{:S(2)}) collective-permute-start(bf16[256,384]{1,0:T(8,128)(2,1)S(1)} %get-tuple-element.94), channel_id=1, source_target_pairs={{0,12},{1,13},{2,14},{3,15},{4,0},{5,1},{6,2},{7,3},{8,4},{9,5},{1... | collective-permute-start | bytes 589832 | tf_op jit(solution)/shard_map/ppermute | solution.py:506
  27.3 6.6 %copy-start.18 = (bf16[400,256]{1,0:T(8,128)(2,1)}, bf16[400,256]{1,0:T(8,128)(2,1)S(1)}, u32[]{:S(2)}) copy-start(bf16[400,256]{1,0:T(8,128)(2,1)S(1)} %collective-permute-done.4.q2) | copy-start | bytes 614404
  27.3 25.0 %collective-permute-start.9 = (bf16[256,384]{1,0:T(8,128)(2,1)S(1)}, bf16[256,384]{1,0:T(8,128)(2,1)S(1)}, u32[]{:S(2)}, u32[]{:S(2)}) collective-permute-start(bf16[256,384]{1,0:T(8,128)(2,1)S(1)} %get-tuple-element.92), channel_id=1, source_target_pairs={{0,4},{1,5},{2,6},{3,7},{4,8},{5,9},{6,10},{7,11},{8,12},{9,13},{1... | collective-permute-start | bytes 589832 | tf_op jit(solution)/shard_map/ppermute | solution.py:506
  33.9 0.7 copy-start.19
  34.5 0.7 copy-start.22
  52.3 4.1 %collective-permute-start.15 = (bf16[3,512,128]{2,1,0:T(8,128)(2,1)}, bf16[3,512,128]{2,1,0:T(8,128)(2,1)S(1)}, u32[]{:S(2)}, u32[]{:S(2)}) collective-permute-start(bf16[3,512,128]{2,1,0:T(8,128)(2,1)} %get-tuple-element.101), channel_id=1, source_target_pairs={{0,1},{1,0},{2,3},{3,2},{4,5},{5,4},{6,7},{7,6},{8,9},{9,8},{10,11... | collective-permute-start | bytes 1179656 | tf_op jit(solution)/shard_map/ppermute | solution.py:546
  52.4 19.2 %collective-permute-start.12 = (bf16[4,192,256]{2,1,0:T(8,128)(2,1)}, bf16[4,192,256]{2,1,0:T(8,128)(2,1)S(1)}, u32[]{:S(2)}, u32[]{:S(2)}) collective-permute-start(bf16[4,192,256]{2,1,0:T(8,128)(2,1)} %get-tuple-element.122.d0), channel_id=1, source_target_pairs={{0,4},{1,5},{2,6},{3,7},{4,8},{5,9},{6,10},{7,11},{8,12},{9,13},{1... | collective-permute-start | bytes 1179656 | tf_op jit(solution)/shard_map/ppermute | solution.py:545
  52.5 19.7 %collective-permute-start.13 = (bf16[4,192,256]{2,1,0:T(8,128)(2,1)}, bf16[4,192,256]{2,1,0:T(8,128)(2,1)S(1)}, u32[]{:S(2)}, u32[]{:S(2)}) collective-permute-start(bf16[4,192,256]{2,1,0:T(8,128)(2,1)} %get-tuple-element.122.d0), channel_id=1, source_target_pairs={{0,8},{1,9},{2,10},{3,11},{4,12},{5,13},{6,14},{7,15},{8,0},{9,1},... | collective-permute-start | bytes 1179656 | tf_op jit(solution)/shard_map/ppermute | solution.py:545
  53.8 20.9 %collective-permute-start.14 = (bf16[4,192,256]{2,1,0:T(8,128)(2,1)}, bf16[4,192,256]{2,1,0:T(8,128)(2,1)S(1)}, u32[]{:S(2)}, u32[]{:S(2)}) collective-permute-start(bf16[4,192,256]{2,1,0:T(8,128)(2,1)} %get-tuple-element.122.d0), channel_id=1, source_target_pairs={{0,12},{1,13},{2,14},{3,15},{4,0},{5,1},{6,2},{7,3},{8,4},{9,5},{1... | collective-permute-start | bytes 1179656 | tf_op jit(solution)/shard_map/ppermute | solution.py:545
  56.3 3.3 %copy-start.15 = (bf16[3,512,128]{2,1,0:T(8,128)(2,1)}, bf16[3,512,128]{2,1,0:T(8,128)(2,1)S(1)}, u32[]{:S(2)}) copy-start(bf16[3,512,128]{2,1,0:T(8,128)(2,1)S(1)} %collective-permute-done.15.core_ref) | copy-start | bytes 1179652
  57.5 8.0 %collective-permute-start.16 = (bf16[3,256,128]{2,1,0:T(8,128)(2,1)S(1)}, bf16[3,256,128]{2,1,0:T(8,128)(2,1)S(1)}, u32[]{:S(2)}, u32[]{:S(2)}) collective-permute-start(bf16[3,256,128]{2,1,0:T(8,128)(2,1)S(1)} %add_convert_fusion), channel_id=1, source_target_pairs={{0,2},{1,3},{2,0},{3,1},{4,6},{5,7},{6,4},{7,5},{8,10},{9,11},{10,... | collective-permute-start | bytes 589832 | tf_op jit(solution)/shard_map/ppermute | solution.py:548
  65.5 0.7 copy-start.23
  66.2 8.6 %copy-start.3 = (bf16[4,192,256]{2,1,0:T(8,128)(2,1)S(1)}, bf16[4,192,256]{2,1,0:T(8,128)(2,1)}, u32[]{:S(2)}) copy-start(bf16[4,192,256]{2,1,0:T(8,128)(2,1)} %get-tuple-element.122.d0) | copy-start | bytes 1179652
  68.5 8.8 %collective-permute-start.18 = (bf16[4,3,64,128]{3,2,1,0:T(8,128)(2,1)}, bf16[4,3,64,128]{3,2,1,0:T(8,128)(2,1)S(1)}, u32[]{:S(2)}, u32[]{:S(2)}) collective-permute-start(bf16[4,3,64,128]{3,2,1,0:T(8,128)(2,1)} %finish_dkv.1.k0), channel_id=1, source_target_pairs={{0,4},{1,5},{2,6},{3,7},{4,8},{5,9},{6,10},{7,11},{8,12},{9,13},{1... | collective-permute-start | bytes 589832 | tf_op jit(solution)/shard_map/ppermute | solution.py:554
  68.5 10.5 %collective-permute-start.19 = (bf16[4,3,64,128]{3,2,1,0:T(8,128)(2,1)}, bf16[4,3,64,128]{3,2,1,0:T(8,128)(2,1)S(1)}, u32[]{:S(2)}, u32[]{:S(2)}) collective-permute-start(bf16[4,3,64,128]{3,2,1,0:T(8,128)(2,1)} %finish_dkv.1.k0), channel_id=1, source_target_pairs={{0,8},{1,9},{2,10},{3,11},{4,12},{5,13},{6,14},{7,15},{8,0},{9,1},... | collective-permute-start | bytes 589832 | tf_op jit(solution)/shard_map/ppermute | solution.py:554
  71.6 5.5 %copy-start.4 = (bf16[4,192,256]{2,1,0:T(8,128)(2,1)}, bf16[4,192,256]{2,1,0:T(8,128)(2,1)S(1)}, u32[]{:S(2)}) copy-start(bf16[4,192,256]{2,1,0:T(8,128)(2,1)S(1)} %collective-permute-done.12.d1) | copy-start | bytes 1179652
  71.6 10.6 %collective-permute-start.20 = (bf16[4,3,64,128]{3,2,1,0:T(8,128)(2,1)}, bf16[4,3,64,128]{3,2,1,0:T(8,128)(2,1)S(1)}, u32[]{:S(2)}, u32[]{:S(2)}) collective-permute-start(bf16[4,3,64,128]{3,2,1,0:T(8,128)(2,1)} %finish_dkv.1.k0), channel_id=1, source_target_pairs={{0,12},{1,13},{2,14},{3,15},{4,0},{5,1},{6,2},{7,3},{8,4},{9,5},{1... | collective-permute-start | bytes 589832 | tf_op jit(solution)/shard_map/ppermute | solution.py:554
  72.2 4.9 %copy-start.5 = (bf16[4,192,256]{2,1,0:T(8,128)(2,1)}, bf16[4,192,256]{2,1,0:T(8,128)(2,1)S(1)}, u32[]{:S(2)}) copy-start(bf16[4,192,256]{2,1,0:T(8,128)(2,1)S(1)} %collective-permute-done.13.d2) | copy-start | bytes 1179652
  74.8 2.4 %copy-start.6 = (bf16[4,192,256]{2,1,0:T(8,128)(2,1)}, bf16[4,192,256]{2,1,0:T(8,128)(2,1)S(1)}, u32[]{:S(2)}) copy-start(bf16[4,192,256]{2,1,0:T(8,128)(2,1)S(1)} %collective-permute-done.14.d3) | copy-start | bytes 1179652
  74.8 7.5 %copy-start.7 = (bf16[4,3,64,128]{3,2,1,0:T(8,128)(2,1)S(1)}, bf16[4,3,64,128]{3,2,1,0:T(8,128)(2,1)}, u32[]{:S(2)}) copy-start(bf16[4,3,64,128]{3,2,1,0:T(8,128)(2,1)} %finish_dkv.1.k0) | copy-start | bytes 589828
  77.1 6.7 %collective-permute-start.17 = (bf16[2,96,768]{2,1,0:T(8,128)(2,1)}, bf16[2,96,768]{2,1,0:T(8,128)(2,1)}, u32[]{:S(2)}, u32[]{:S(2)}) collective-permute-start(bf16[2,96,768]{2,1,0:T(8,128)(2,1)} %get-tuple-element.115), channel_id=1, source_target_pairs={{0,1},{1,0},{2,3},{3,2},{4,5},{5,4},{6,7},{7,6},{8,9},{9,8},{10,11... | collective-permute-start | bytes 884744 | tf_op jit(solution)/shard_map/ppermute | solution.py:514
  77.3 6.4 %copy-start.8 = (bf16[4,3,64,128]{3,2,1,0:T(8,128)(2,1)}, bf16[4,3,64,128]{3,2,1,0:T(8,128)(2,1)S(1)}, u32[]{:S(2)}) copy-start(bf16[4,3,64,128]{3,2,1,0:T(8,128)(2,1)S(1)} %collective-permute-done.18.k1) | copy-start | bytes 589828
  79.0 4.7 %copy-start.9 = (bf16[4,3,64,128]{3,2,1,0:T(8,128)(2,1)}, bf16[4,3,64,128]{3,2,1,0:T(8,128)(2,1)S(1)}, u32[]{:S(2)}) copy-start(bf16[4,3,64,128]{3,2,1,0:T(8,128)(2,1)S(1)} %collective-permute-done.19.k2) | copy-start | bytes 589828
  82.2 1.5 %copy-start.10 = (bf16[4,3,64,128]{3,2,1,0:T(8,128)(2,1)}, bf16[4,3,64,128]{3,2,1,0:T(8,128)(2,1)S(1)}, u32[]{:S(2)}) copy-start(bf16[4,3,64,128]{3,2,1,0:T(8,128)(2,1)S(1)} %collective-permute-done.20.k3) | copy-start | bytes 589828
  83.7 2.2 %collective-permute-start.21 = (bf16[2,96,1664]{2,1,0:T(8,128)(2,1)S(1)}, bf16[2,96,1664]{2,1,0:T(8,128)(2,1)S(1)}, u32[]{:S(2)}, u32[]{:S(2)}) collective-permute-start(bf16[2,96,1664]{2,1,0:T(8,128)(2,1)S(1)} %get-tuple-element.120), channel_id=1, source_target_pairs={{0,1},{1,0},{2,3},{3,2},{4,5},{5,4},{6,7},{7,6},{8,9},{9,8},{10,11... | collective-permute-start | bytes 1916936 | tf_op jit(solution)/shard_map/ppermute | solution.py:514
  86.0 14.3 %collective-permute-start.22 = (bf16[96,1664]{1,0:T(8,128)(2,1)S(1)}, bf16[96,1664]{1,0:T(8,128)(2,1)S(1)}, u32[]{:S(2)}, u32[]{:S(2)}) collective-permute-start(bf16[96,1664]{1,0:T(8,128)(2,1)S(1)} %fusion.1), channel_id=1, source_target_pairs={{0,2},{1,3},{2,0},{3,1},{4,6},{5,7},{6,4},{7,5},{8,10},{9,11},{10,... | collective-permute-start | bytes 958472 | tf_op jit(solution)/shard_map/ppermute | solution.py:563
  86.2 14.2 %collective-permute-start.23 = (bf16[96,768]{1,0:T(8,128)(2,1)S(1)}, bf16[96,768]{1,0:T(8,128)(2,1)S(1)}, u32[]{:S(2)}, u32[]{:S(2)}) collective-permute-start(bf16[96,768]{1,0:T(8,128)(2,1)S(1)} %fusion.3), channel_id=1, source_target_pairs={{0,2},{1,3},{2,0},{3,1},{4,6},{5,7},{6,4},{7,5},{8,10},{9,11},{10,... | collective-permute-start | bytes 442376 | tf_op jit(solution)/shard_map/ppermute | solution.py:562
  125.4 8.7 %copy-start.26 = (bf16[192,256]{1,0:T(8,128)(2,1)S(1)}, bf16[192,256]{1,0:T(8,128)(2,1)}, u32[]{:S(2)}) copy-start(bf16[192,256]{1,0:T(8,128)(2,1)} %get-tuple-element.128) | copy-start | bytes 294916
  125.4 9.2 %copy-start.25 = (bf16[192,256]{1,0:T(8,128)(2,1)S(1)}, bf16[192,256]{1,0:T(8,128)(2,1)}, u32[]{:S(2)}) copy-start(bf16[192,256]{1,0:T(8,128)(2,1)} %get-tuple-element.129) | copy-start | bytes 294916
  125.4 11.2 %copy-start.24 = (bf16[192,256]{1,0:T(8,128)(2,1)S(1)}, bf16[192,256]{1,0:T(8,128)(2,1)}, u32[]{:S(2)}) copy-start(bf16[192,256]{1,0:T(8,128)(2,1)} %get-tuple-element.130) | copy-start | bytes 294916
  125.4 16.5 %copy-start.14 = (bf16[192,256]{1,0:T(8,128)(2,1)S(1)}, bf16[192,256]{1,0:T(8,128)(2,1)}, u32[]{:S(2)}) copy-start(bf16[192,256]{1,0:T(8,128)(2,1)} %get-tuple-element.84) | copy-start | bytes 294916
  125.5 4.3 %collective-permute-start.27 = (bf16[24,1280]{1,0:T(8,128)(2,1)S(1)}, bf16[24,1280]{1,0:T(8,128)(2,1)S(1)}, u32[]{:S(2)}, u32[]{:S(2)}) collective-permute-start(bf16[24,1280]{1,0:T(8,128)(2,1)S(1)} %reduce_sum.12), channel_id=1, source_target_pairs={{0,128},{16,144},{32,160},{48,176},{64,192},{80,208},{96,224},{112... | collective-permute-start | bytes 184328 | tf_op jit(solution)/shard_map/ppermute | solution.py:581
  130.6 16.0 %all-to-all-start.1 = ((bf16[8,24,1152]{2,1,0:T(8,128)(2,1)}), bf16[8,24,1152]{2,1,0:T(8,128)(2,1)S(1)}, u32[]{:S(2)}, u32[]{:S(2)}) async-start(bf16[8,24,1152]{2,1,0:T(8,128)(2,1)} %broadcast_in_dim.8), calls=%async_computation.1 | async-start | bytes 884736 | tf_op jit(solution)/shard_map/all_to_all | solution.py:585
  134.1 4.7 %collective-permute-start.24 = (bf16[192,256]{1,0:T(8,128)(2,1)S(1)}, bf16[192,256]{1,0:T(8,128)(2,1)S(1)}, u32[]{:S(2)}, u32[]{:S(2)}) collective-permute-start(bf16[192,256]{1,0:T(8,128)(2,1)S(1)} %copy-done.26), channel_id=1, source_target_pairs={{0,12},{1,13},{2,14},{3,15},{4,0},{5,1},{6,2},{7,3},{8,4},{9,5},{1... | collective-permute-start | bytes 294920 | tf_op jit(solution)/shard_map/ppermute | solution.py:575
  134.6 6.1 %collective-permute-start.25 = (bf16[192,256]{1,0:T(8,128)(2,1)S(1)}, bf16[192,256]{1,0:T(8,128)(2,1)S(1)}, u32[]{:S(2)}, u32[]{:S(2)}) collective-permute-start(bf16[192,256]{1,0:T(8,128)(2,1)S(1)} %copy-done.25), channel_id=1, source_target_pairs={{0,8},{1,9},{2,10},{3,11},{4,12},{5,13},{6,14},{7,15},{8,0},{9,1},... | collective-permute-start | bytes 294920 | tf_op jit(solution)/shard_map/ppermute | solution.py:575
  136.6 5.4 %collective-permute-start.26 = (bf16[192,256]{1,0:T(8,128)(2,1)S(1)}, bf16[192,256]{1,0:T(8,128)(2,1)S(1)}, u32[]{:S(2)}, u32[]{:S(2)}) collective-permute-start(bf16[192,256]{1,0:T(8,128)(2,1)S(1)} %copy-done.24), channel_id=1, source_target_pairs={{0,4},{1,5},{2,6},{3,7},{4,8},{5,9},{6,10},{7,11},{8,12},{9,13},{1... | collective-permute-start | bytes 294920 | tf_op jit(solution)/shard_map/ppermute | solution.py:575
